TPU v7x, 256 devices: a whole 4x4x8 slice. The times are simulated.
256 devices in a mesh: sec: 32 (over x, z), term: 8 (over y, core).
Axes of the slice: x: 4, y: 4, z: 8, core: 2. Of those that a mesh axis runs over, the one named last changes fastest.
Arguments:
- psi: bfloat16 [256, 384, 384], P('sec'), may hold values from -1.5 to 1.5
- left_ops: bfloat16 [16, 256, 384, 384], P('term', 'sec'), may hold values from -0.3125 to 0.3125
- right_ops: bfloat16 [16, 256, 384, 384], P('term', 'sec'), may hold values from -0.3125 to 0.3125
- pair_src: int32 [16, 256], P('term'), may hold values from 0 to 255, each once within a row
- widths: int32 [2, 256], P(None, 'sec'), may hold values from 64 to 384, as said below
Outputs:
- sigma: float32 [256, 384, 384], P('sec', None, 'term')
Inputs may be any that keep to these rules, and one draw needn't show every extreme that they name: Each entry lies between 64 and 384; in every draw all sectors of some one index of sec have both widths equal to 384. `pair_src`: each row is a permutation of the 256 sectors.
All inputs are finite; a program needn't handle non-finite values.
Results may differ from a plain program's by a relative error of at most 0.015.
Values may be sent and summed in bfloat16 or wider, within the bound.
A program may use at most 64 MiB of HBM per device.

v0:
```python
import jax
import jax.numpy as jnp
from jax import lax
from jax.sharding import PartitionSpec as P


def contract(left_block, right_block, masked):
    half = jnp.einsum(
        "kij,kjl->kil", left_block, masked, preferred_element_type=jnp.float32
    ).astype(jnp.bfloat16)
    return jnp.einsum("kil,kml->kim", half, right_block, preferred_element_type=jnp.float32).astype(
        jnp.bfloat16
    )


def shards(psi, left_ops, right_ops, pair_src, widths):
    size = psi.shape[1]
    groups_here = left_ops.shape[0]
    line = jnp.arange(size, dtype=jnp.int32)
    keep = (line[None, :, None] < widths[0][:, None, None]) & (
        line[None, None, :] < widths[1][:, None, None]
    )
    masked = jnp.where(keep, psi, jnp.zeros_like(psi))
    images = jnp.stack(
        [contract(left_ops[group], right_ops[group], masked) for group in range(groups_here)]
    )
    regrouped = lax.all_to_all(images, "sec", split_axis=2, concat_axis=1, tiled=True)
    partial_sum = jnp.take(regrouped[0], pair_src[0], axis=0).astype(jnp.float32)
    group = 1
    partial_sum = partial_sum + jnp.take(regrouped[group], pair_src[group], axis=0).astype(
        jnp.float32
    )
    window_part = partial_sum.astype(jnp.bfloat16)
    returned = lax.all_to_all(window_part, "sec", split_axis=0, concat_axis=1, tiled=True)
    summed = lax.psum_scatter(
        returned.astype(jnp.float32).astype(jnp.bfloat16), "term", scatter_dimension=2, tiled=True
    ).astype(jnp.float32)
    col_width = summed.shape[2]
    columns = lax.axis_index("term") * col_width + jnp.arange(col_width, dtype=jnp.int32)
    out_keep = (line[None, :, None] < widths[0][:, None, None]) & (
        columns[None, None, :] < widths[1][:, None, None]
    )
    return jnp.where(out_keep, summed, jnp.zeros_like(summed))


def solution(mesh):
    return jax.shard_map(
        shards,
        mesh=mesh,
        in_specs=(
            P("sec", None, None),
            P("term", "sec", None, None),
            P("term", "sec", None, None),
            P("term", None),
            P(None, "sec"),
        ),
        out_specs=P("sec", None, "term"),
        check_vma=False,
    )
```

profile of v0, /device:TPU:1, one launch (start us, length us, event | category | flops | bytes accessed | tf_op | source)
XLA Modules:
  0.0 295.3 jit_solution(8555940814681918386)
XLA Ops:
  6.5 0.8 slice_bitcast_fusion.1
  7.3 0.1 iota_compare_fusion
  7.4 6.8 %convert_bitcast_fusion.1 = bf16[1,8,384,384]{3,2,1,0:T(8,128)(2,1)S(1)} fusion(bf16[2,8,384,384]{3,2,1,0:T(8,128)(2,1)} %param.9, bf16[2,8,384,384]{3,2,1,0:T(8,128)(2,1)} %param.8, bf16[8,384,384]{2,1,0:T(8,128)(2,1)} %param.7, pred[8,384]{1,0:T(8,128)(4,1)S(1)} %get-tuple-element.12, pred[8,384]{1,0:T(8,128)(4,1)S(1)} %get-tuple-element.13), kind=kOutput, calls=%fused_computation.19 | convolution fusion | flops 1816657920 | bytes 9443328 | tf_op jit(solution)/shard_map/kil,kml->kim/dot_general | solution.py:11
  14.2 8.2 %convert_bitcast_fusion = bf16[1,8,384,384]{3,2,1,0:T(8,128)(2,1)} fusion(bf16[2,8,384,384]{3,2,1,0:T(8,128)(2,1)} %param.9, bf16[2,8,384,384]{3,2,1,0:T(8,128)(2,1)} %param.8, bf16[8,384,384]{2,1,0:T(8,128)(2,1)} %param.7, pred[8,384]{1,0:T(8,128)(4,1)S(1)} %get-tuple-element.12, pred[8,384]{1,0:T(8,128)(4,1)S(1)} %get-tuple-element.13), kind=kOutput, calls=%fused_computation.15 | convolution fusion | flops 1816657920 | bytes 9443328 | tf_op jit(solution)/shard_map/kil,kml->kim/dot_general | solution.py:11
  22.4 2.2 pad_maximum_fusion
  24.6 5.0 %copy.29 = bf16[2,8,384,384]{3,1,0,2:T(8,128)(2,1)} copy(bf16[2,8,384,384]{3,2,1,0:T(8,128)(2,1)S(1)} %pad_maximum_fusion) | data formatting | bytes 9437184 | tf_op jit(solution)/shard_map/stack | solution.py:24
  29.6 0.0 copy-start
  29.6 12.1 %all-to-all-start = ((bf16[2,8,384,384]{3,1,0,2:T(8,128)(2,1)}), bf16[2,8,384,384]{3,1,0,2:T(8,128)(2,1)}, u32[]{:S(2)}, u32[]{:S(2)}) async-start(bf16[2,8,384,384]{3,1,0,2:T(8,128)(2,1)} %copy.29), calls=%async_computation | async-start | bytes 9437184 | tf_op jit(solution)/shard_map/all_to_all | solution.py:27
  41.7 0.2 reduce-scatter.2.cloned.1.call-start
  42.0 0.0 copy-done
  42.0 103.1 %all-to-all-done = bf16[2,8,384,384]{3,1,0,2:T(8,128)(2,1)} async-done(((bf16[2,8,384,384]{3,1,0,2:T(8,128)(2,1)}), bf16[2,8,384,384]{3,1,0,2:T(8,128)(2,1)}, u32[]{:S(2)}, u32[]{:S(2)}) %all-to-all-start) | async-done | bytes 4718624 | tf_op jit(solution)/shard_map/all_to_all | solution.py:27
  145.2 2.8 copy.30
  148.0 0.5 fusion.42
  148.4 0.3 copy.47
  148.8 3.2 %copy.32 = bf16[256,12,384]{2,1,0:T(8,128)(2,1)} copy(bf16[256,12,384]{2,0,1:T(8,128)(2,1)S(1)} %bitcast.53) | data formatting | bytes 4718592 | tf_op jit(solution)/shard_map/squeeze | solution.py:28
  151.9 0.3 copy.46
  152.3 3.1 %copy.34 = bf16[256,12,384]{2,1,0:T(8,128)(2,1)} copy(bf16[256,12,384]{2,0,1:T(8,128)(2,1)S(1)} %bitcast.54) | data formatting | bytes 4718592 | tf_op jit(solution)/shard_map/squeeze | solution.py:30
  155.4 3.2 %gather_fusion = bf16[256,12,384]{2,1,0:T(8,128)(2,1)S(1)} fusion(bf16[256,12,384]{2,1,0:T(8,128)(2,1)} %copy.32, s32[1024]{0:T(1024)S(1)} %pad_clamp_fusion.1), kind=kCustom, calls=%fused_computation.clone | custom fusion | bytes 4719616 | tf_op jit(solution)/shard_map/jit(_take)/gather | solution.py:28
  158.6 4.6 %gather_fusion.1 = bf16[256,12,384]{2,1,0:T(8,128)(2,1)} fusion(bf16[256,12,384]{2,1,0:T(8,128)(2,1)} %copy.34, s32[1024]{0:T(1024)S(1)} %pad_clamp_fusion), kind=kCustom, calls=%fused_computation.1.clone | custom fusion | bytes 4719616 | tf_op jit(solution)/shard_map/jit(_take)/gather | solution.py:30
  163.2 3.6 %add_convert_fusion = bf16[256,12,384]{2,1,0:T(8,128)(2,1)S(1)} fusion(bf16[256,12,384]{2,1,0:T(8,128)(2,1)} %gather_fusion.1, bf16[256,12,384]{2,1,0:T(8,128)(2,1)S(1)} %gather_fusion, pred[256]{0:T(512)(128)(4,1)S(1)} %get-tuple-element.14, pred[256]{0:T(512)(128)(4,1)S(1)} %get-tuple-element.15), kind=kLoop, calls=%fused_computation.2 | loop fusion | flops 7077888 | bytes 7078400 | tf_op jit(solution)/shard_map/convert_element_type | solution.py:33
  166.8 80.5 %all_to_all.33 = bf16[256,12,384]{2,1,0:T(8,128)(2,1)S(1)} all-to-all(bf16[256,12,384]{2,1,0:T(8,128)(2,1)S(1)} %add_convert_fusion), channel_id=1, replica_groups=mesh['sec'=32,'term'=8] {'sec'}, dimensions={0} | all-to-all | bytes 4718592 | tf_op jit(solution)/shard_map/all_to_all | solution.py:34
  247.3 0.6 copy.36
  248.0 3.3 %copy.37 = bf16[8,384,384]{1,0,2:T(8,128)(2,1)} copy(bf16[8,384,384]{2,0,1:T(8,128)(2,1)S(1)} %bitcast.55) | data formatting | bytes 4718592 | tf_op jit(solution)/shard_map/all_to_all | solution.py:34
  251.2 0.0 reduce-scatter.2.cloned.1.call-update
  251.3 0.1 broadcast_compare_fusion
  251.3 35.1 %reduce-scatter.2.cloned.1.call-done = bf16[8,384,48]{1,0,2:T(8,128)(2,1)} async-done(((bf16[8,384,384]{1,0,2:T(8,128)(2,1)}), bf16[8,384,48]{1,0,2:T(8,128)(2,1)}) %reduce-scatter.2.cloned.1.call-update) | async-done | bytes 294928 | tf_op jit(solution)/shard_map/reduce_scatter | solution.py:35
  286.4 1.1 convert_select_fusion
  287.6 0.9 copy.38
  (7 shorter events, 0.0 us)
Async XLA Ops:
  29.6 12.4 %copy-start = (s32[2,256]{1,0:T(2,128)S(1)}, s32[2,256]{1,0:T(2,128)}, u32[]{:S(2)}) copy-start(s32[2,256]{1,0:T(2,128)} %param.10) | copy-start | bytes 6148
  29.6 115.5 %all-to-all-start = ((bf16[2,8,384,384]{3,1,0,2:T(8,128)(2,1)}), bf16[2,8,384,384]{3,1,0,2:T(8,128)(2,1)}, u32[]{:S(2)}, u32[]{:S(2)}) async-start(bf16[2,8,384,384]{3,1,0,2:T(8,128)(2,1)} %copy.29), calls=%async_computation | async-start | bytes 9437184 | tf_op jit(solution)/shard_map/all_to_all | solution.py:27
  41.7 244.7 %reduce-scatter.2.cloned.1.call-start = ((), (), s32[]{:S(2)}) async-start(), calls=%async_computation.3 | async-start | bytes 2654208 | tf_op jit(solution)/shard_map/reduce_scatter | solution.py:35
Sparse Core Ops, SparseCore 0:
  251.4 35.0 reduce-scatter.1
where the time goes:
time: 298 us; the launch traced here: 295 us
  waiting for transfers between devices  138 us (46%)
  blocking collectives  80.5 us (27%)
  local copies, waits for them, and re-layouts  28.6 us (10%)
  matrix products  15 us (5%)
  between operations  13.5 us (5%)
  starting transfers between devices  12.3 us (4%)
  other arithmetic  7.06 us (2%)
    all_to_all x1, waiting for transfers between devices, shards(): lax.all_to_all(images, 'sec', split_axis=2, concat_axis=1, tiled=True)  103 us
    all_to_all x1, blocking collectives, shards(): lax.all_to_all(window_part, 'sec', split_axis=0, concat_axis=1, tiled=True)  80.5 us
    reduce_scatter x1, waiting for transfers between devices, shards(): lax.psum_scatter(returned.astype(jnp.float32).astype(jnp.bfloat16), 'term...  35.1 us
    dot_general x2, matrix products, contract(): jnp.einsum('kil,kml->kim', half, right_block, preferred_element_type=jnp....  15 us
    all_to_all x1, starting transfers between devices, shards(): lax.all_to_all(images, 'sec', split_axis=2, concat_axis=1, tiled=True)  12.1 us
  transfers between devices with their start and end apart: 2, of which 2 were waited for; matrix products, arithmetic and copies ran while one was open for 0% of the time, Pallas kernels for 0%

commit v1 on v0

v1 whole, which is shorter than its diff:
```python
import functools

import jax
import jax.numpy as jnp
from jax import lax
from jax.experimental import pallas as pl
from jax.experimental.pallas import tpu as pltpu
from jax.sharding import PartitionSpec as P

NX, NY, NZ, NC = 4, 4, 8, 2
PIECES = 3
HALVES = 2
SLOTS = NX * NY
SECTORS_HERE = 8
PER_HALF = SECTORS_HERE // HALVES
X_PART = NX // NC
STEPS = NZ // 2
EMPTY = SLOTS * SECTORS_HERE
MESH = pl.DeviceIdType.MESH


def device(x, y, z, c):
    return (x * NZ + z, y * NC + c)


def rows_of(ref, index, start, count):
    low = start // 16 * 16
    high = min(-(-(start + count) // 16) * 16, ref.shape[-2])
    value = ref[index + (slice(low, high), slice(None))].astype(jnp.float32)
    return value[start - low : start - low + count]


def kernel(
    slot_in, widths, psi, left, right, out,
    psi_v, left_v, right_v, sends, got0, got1, got2, slot_v, slot_s,
    give, take, own, up_out, up_in, down_out, down_in, done, final,
    load_sem, slot_sem, slot_send, spread_send, spread_recv, core_send, core_recv,
    up_send, up_recv, down_send, down_recv, final_send, final_recv,
):
    got = (got0, got1, got2)[:PIECES]
    sec, term = lax.axis_index("sec"), lax.axis_index("term")
    x, z = lax.div(sec, NZ), lax.rem(sec, NZ)
    y, c = lax.div(term, NC), lax.rem(term, NC)
    me = y * NX + x
    size = psi_v.shape[-1]
    rows = size // SLOTS
    lanes = size // PIECES
    moves = [(dx, dy) for dx in range(NX) for dy in range(NY) if (dx, dy) != (0, 0)]
    moves.sort(key=lambda m: -(min(m[0], NX - m[0]) + min(m[1], NY - m[1])))

    def shifted(value, by, count):
        return lax.rem(value + (by % count), count)

    barrier = pltpu.get_barrier_semaphore()
    others = [device(shifted(x, dx, NX), shifted(y, dy, NY), z, c) for dx, dy in moves]
    others += [device(shifted(x, dx, NX), y, z, 1 - c) for dx in range(NX)]
    others += [device(x, y, shifted(z, 1, NZ), c), device(x, y, shifted(z, -1, NZ), c)]
    for other in others:
        pl.semaphore_signal(barrier, inc=1, device_id=other, device_id_type=MESH)

    def loads(k):
        return (
            pltpu.make_async_copy(psi.at[k], psi_v.at[k], load_sem.at[0, k]),
            pltpu.make_async_copy(right.at[:, k], right_v.at[:, k], load_sem.at[1, k]),
            pltpu.make_async_copy(left.at[:, k], left_v.at[:, k], load_sem.at[2, k]),
        )

    for k in range(SECTORS_HERE):
        for copy in loads(k):
            copy.start()
    for piece in range(PIECES):
        got[piece][EMPTY] = jnp.zeros(got[piece].shape[1:], got[piece].dtype)

    def images(piece, half):
        def one(inner, _):
            k = half * PER_HALF + inner
            if piece == 0:
                for copy in loads(k):
                    copy.wait()
                keep = (lax.broadcasted_iota(jnp.int32, (size, size), 0) < widths[0, k]) & (
                    lax.broadcasted_iota(jnp.int32, (size, size), 1) < widths[1, k]
                )
                psi_v[k] = jnp.where(keep, psi_v[k].astype(jnp.float32), 0.0).astype(jnp.bfloat16)
            block = []
            for group in range(2):
                part = jnp.dot(
                    left_v[group, k, piece * lanes : (piece + 1) * lanes, :],
                    psi_v[k],
                    preferred_element_type=jnp.float32,
                ).astype(jnp.bfloat16)
                block.append(
                    lax.dot_general(
                        right_v[group, k], part, (((1,), (1,)), ((), ())),
                        preferred_element_type=jnp.float32,
                    )
                )
            for slot in range(SLOTS):
                at = slice(slot * rows, (slot + 1) * rows)
                sends[piece, slot, k] = jnp.concatenate([block[0][at], block[1][at]], 0).astype(
                    jnp.bfloat16
                )
            return 0

        lax.fori_loop(0, PER_HALF, one, 0)

    def spread(piece, half):
        first = half * PER_HALF
        place = pl.ds(half * (SLOTS * PER_HALF) + me * PER_HALF, PER_HALF)
        for dx, dy in moves:
            xd, yd = shifted(x, dx, NX), shifted(y, dy, NY)
            pltpu.make_async_remote_copy(
                src_ref=sends.at[piece, yd * NX + xd, first : first + PER_HALF],
                dst_ref=got[piece].at[place],
                send_sem=spread_send.at[piece],
                recv_sem=spread_recv.at[piece],
                device_id=device(xd, yd, z, c),
                device_id_type=MESH,
            ).start()
        pltpu.make_async_copy(
            sends.at[piece, me, first : first + PER_HALF], got[piece].at[place], spread_recv.at[piece]
        ).start()

    def slot_copy(dy):
        return pltpu.make_async_remote_copy(
            src_ref=slot_in,
            dst_ref=slot_v.at[y],
            send_sem=slot_send.at[dy],
            recv_sem=slot_sem.at[0],
            device_id=device(x, shifted(y, dy, NY), z, c),
            device_id_type=MESH,
        )

    def gather(piece, part, to):
        first = part * (to.shape[1] * 2)

        def pair(p, _):
            both = []
            for which in range(2):
                total = jnp.zeros((rows, lanes), jnp.float32)
                for yy in range(NY):
                    for group in range(2):
                        slot = slot_s[yy, group, first + 2 * p + which]
                        total = total + rows_of(got[piece], (slot,), group * rows, rows)
                both.append(total)
            to[piece, p] = jnp.concatenate(both, 0).astype(to.dtype)
            return 0

        lax.fori_loop(0, to.shape[1], pair, 0)

    def core_copy(piece):
        return pltpu.make_async_remote_copy(
            src_ref=give.at[piece],
            dst_ref=take.at[piece],
            send_sem=core_send.at[piece],
            recv_sem=core_recv.at[piece],
            device_id=device(x, y, z, 1 - c),
            device_id_type=MESH,
        )

    def held(piece, part, zd):
        at = pl.ds(part * (NZ * PER_HALF) + zd * PER_HALF, PER_HALF)
        return own[piece, at] + take[piece, at].astype(jnp.float32)

    def z_copy(piece, step, way):
        source, target = (up_out, up_in) if way > 0 else (down_out, down_in)
        out_sem, in_sem = (up_send, up_recv) if way > 0 else (down_send, down_recv)
        at = (piece, step) if step > 0 else (piece, step, 0 if way > 0 else 1)
        return pltpu.make_async_remote_copy(
            src_ref=source.at[at],
            dst_ref=target.at[at],
            send_sem=out_sem.at[piece, step],
            recv_sem=in_sem.at[piece, step],
            device_id=device(x, y, shifted(z, way, NZ), c),
            device_id_type=MESH,
        )

    def parts_at(step, way):
        return range(X_PART) if step > 0 else ((0,) if way > 0 else (1,))

    def chain(piece):
        for step in range(STEPS):
            for way in (1, -1):
                source, target = (up_out, up_in) if way > 0 else (down_out, down_in)
                if step > 0:
                    z_copy(piece, step - 1, way).wait_recv()
                zd = shifted(z, way * (STEPS - step), NZ)
                for part in parts_at(step, way):
                    value = held(piece, part, zd)
                    if step > 0 and part in parts_at(step - 1, way):
                        value = value + target[piece, step - 1, part].astype(jnp.float32)
                    source[piece, step, part] = value.astype(jnp.bfloat16)
                z_copy(piece, step, way).start()

    def final_copies(piece, part):
        xd = c * X_PART + part
        place = final.at[piece, lax.rem(x, X_PART)]
        there = pltpu.make_async_remote_copy(
            src_ref=done.at[piece, part],
            dst_ref=place,
            send_sem=final_send.at[piece, part],
            recv_sem=final_recv.at[piece],
            device_id=device(xd, y, z, lax.div(x, X_PART)),
            device_id_type=MESH,
        )
        here = pltpu.make_async_copy(done.at[piece, part], place, final_recv.at[piece])
        return xd, there, here

    def finish(piece):
        last = STEPS - 1
        for way in (1, -1):
            z_copy(piece, last, way).wait_recv()
        for part in range(X_PART):
            value = held(piece, part, z)
            if part in parts_at(last, 1):
                value = value + up_in[piece, last, part].astype(jnp.float32)
            if part in parts_at(last, -1):
                value = value + down_in[piece, last, part].astype(jnp.float32)
            done[piece, part] = value.astype(jnp.bfloat16)
            xd, there, here = final_copies(piece, part)

            @pl.when(xd != x)
            def _():
                there.start()

            @pl.when(xd == x)
            def _():
                here.start()

    def reduce_piece(piece):
        pltpu.make_async_copy(
            got[piece].at[0:EMPTY], got[piece].at[0:EMPTY], spread_recv.at[piece]
        ).wait()
        gather(piece, 1 - c, give)
        core_copy(piece).start()
        gather(piece, c, own)
        core_copy(piece).wait_recv()
        chain(piece)
        finish(piece)

    images(0, 0)
    pl.semaphore_wait(barrier, len(others))
    for dy in range(1, NY):
        slot_copy(dy).start()
    pltpu.make_async_copy(slot_in, slot_v.at[y], slot_sem.at[0]).start()
    units = [(piece, half) for piece in range(PIECES) for half in range(HALVES)]
    for unit, following in zip(units, units[1:] + [None]):
        spread(*unit)
        if following is not None:
            images(*following)
    pltpu.make_async_copy(slot_v, slot_v, slot_sem.at[0]).wait()
    to_scalar = pltpu.make_async_copy(slot_v, slot_s, slot_sem.at[1])
    to_scalar.start()
    to_scalar.wait()
    for piece in range(PIECES):
        reduce_piece(piece)
    for piece in range(PIECES):
        pltpu.make_async_copy(final.at[piece], final.at[piece], final_recv.at[piece]).wait()
        for sector in range(SECTORS_HERE):
            for part in range(X_PART):
                out[
                    sector, part * rows : (part + 1) * rows, piece * lanes : (piece + 1) * lanes
                ] = rows_of(final, (piece, part, sector // 2), sector % 2 * rows, rows)

    for dy in range(1, NY):
        slot_copy(dy).wait_send()
    for piece in range(PIECES):
        sent = sends.at[piece, 0 : SLOTS - 1]
        pltpu.make_async_copy(sent, sent, spread_send.at[piece]).wait()
        core_copy(piece).wait_send()
        for step in range(STEPS):
            for way in (1, -1):
                z_copy(piece, step, way).wait_send()
        for part in range(X_PART):
            xd, there, _ = final_copies(piece, part)

            @pl.when(xd != x)
            def _():
                there.wait_send()


def shards(psi, left_ops, right_ops, pair_src, widths):
    size = psi.shape[1]
    targets = pair_src.shape[1]
    rows, lanes = size // SLOTS, size // PIECES
    sec, term = lax.axis_index("sec"), lax.axis_index("term")
    z, y = sec % NZ, term // NC
    here = pair_src // SECTORS_HERE % NZ == z
    x_from, inner = pair_src // (SECTORS_HERE * NZ), pair_src % SECTORS_HERE
    slot = (inner // PER_HALF) * (SLOTS * PER_HALF) + (y * NX + x_from) * PER_HALF + inner % PER_HALF
    slot = jnp.pad(jnp.where(here, slot, EMPTY).astype(jnp.int32), ((0, 6), (0, 0)))

    bf, block = jnp.bfloat16, (2 * rows, lanes)
    half_targets = targets // NC // 2
    ring = pltpu.VMEM((PIECES, STEPS, X_PART, PER_HALF) + block, bf)
    scratch = [
        pltpu.VMEM(psi.shape, bf),
        pltpu.VMEM(left_ops.shape, bf),
        pltpu.VMEM(right_ops.shape, bf),
        pltpu.VMEM((PIECES, SLOTS, SECTORS_HERE) + block, bf),
        *[pltpu.VMEM((EMPTY + 1,) + block, bf) for _ in range(3)],
        pltpu.VMEM((NY,) + slot.shape, jnp.int32),
        pltpu.SMEM((NY,) + slot.shape, jnp.int32),
        pltpu.VMEM((PIECES, half_targets) + block, bf),
        pltpu.VMEM((PIECES, half_targets) + block, bf),
        pltpu.VMEM((PIECES, half_targets) + block, jnp.float32),
        ring, ring, ring, ring,
        pltpu.VMEM((PIECES, X_PART, PER_HALF) + block, bf),
        pltpu.VMEM((PIECES, X_PART, PER_HALF) + block, bf),
    ]
    dma = pltpu.SemaphoreType.DMA
    scratch += [
        dma((3, SECTORS_HERE)), dma((2,)), dma((NY,)), dma((PIECES,)), dma((PIECES,)),
        dma((PIECES,)), dma((PIECES,)),
        dma((PIECES, STEPS)), dma((PIECES, STEPS)), dma((PIECES, STEPS)), dma((PIECES, STEPS)),
        dma((PIECES, X_PART)), dma((PIECES,)),
    ]
    summed = pl.pallas_call(
        kernel,
        out_shape=jax.ShapeDtypeStruct((SECTORS_HERE, X_PART * rows, size), jnp.float32),
        in_specs=[
            pl.BlockSpec(memory_space=pltpu.VMEM),
            pl.BlockSpec(memory_space=pltpu.SMEM),
            pl.BlockSpec(memory_space=pl.ANY),
            pl.BlockSpec(memory_space=pl.ANY),
            pl.BlockSpec(memory_space=pl.ANY),
        ],
        out_specs=pl.BlockSpec(memory_space=pltpu.VMEM),
        scratch_shapes=scratch,
        compiler_params=pltpu.CompilerParams(
            collective_id=0, has_side_effects=True, vmem_limit_bytes=56 * 1024 * 1024
        ),
        cost_estimate=pl.CostEstimate(
            flops=64 * size**3, bytes_accessed=40 * size * size * 2, transcendentals=0
        ),
    )(slot, widths, psi, left_ops, right_ops)

    summed = jnp.swapaxes(summed, 1, 2)
    line = jnp.arange(size, dtype=jnp.int32)
    columns = term * (X_PART * rows) + jnp.arange(X_PART * rows, dtype=jnp.int32)
    keep = (line[None, :, None] < widths[0][:, None, None]) & (
        columns[None, None, :] < widths[1][:, None, None]
    )
    return jnp.where(keep, summed, jnp.zeros_like(summed))


def solution(mesh):
    return jax.shard_map(
        shards,
        mesh=mesh,
        in_specs=(
            P("sec", None, None),
            P("term", "sec", None, None),
            P("term", "sec", None, None),
            P("term", None),
            P(None, "sec"),
        ),
        out_specs=P("sec", None, "term"),
        check_vma=False,
    )
```

time: 298 us -> 108 us (0.36)
  waiting for transfers between devices: 138 us -> 0 us
  Pallas kernels: 0 us -> 104 us
  blocking collectives: 80.5 us -> 0 us
  local copies, waits for them, and re-layouts: 28.6 us -> 0.61 us
  matrix products: 15 us -> 0 us
  between operations: 13.5 us -> 0.04 us
  starting transfers between devices: 12.3 us -> 0 us
  other arithmetic: 7.06 us -> 2.87 us
    pallas_call x0 -> x1, Pallas kernels: none -> 104 us  [shards(): pl.pallas_call(kernel, out_shape=jax.ShapeDtypeStruct((SECTORS_HERE, X_PA...]
    all_to_all x1 -> x0, waiting for transfers between devices: 103 us -> none  [shards(): lax.all_to_all(images, 'sec', split_axis=2, concat_axis=1, tiled=True)]
    all_to_all x1 -> x0, blocking collectives: 80.5 us -> none  [shards(): lax.all_to_all(window_part, 'sec', split_axis=0, concat_axis=1, tiled=True)]
    reduce_scatter x1 -> x0, waiting for transfers between devices: 35.1 us -> none  [shards(): lax.psum_scatter(returned.astype(jnp.float32).astype(jnp.bfloat16), 'term...]
    dot_general x2 -> x0, matrix products: 15 us -> none  [contract(): jnp.einsum('kil,kml->kim', half, right_block, preferred_element_type=jnp....]
    all_to_all x1 -> x0, starting transfers between devices: 12.1 us -> none  [shards(): lax.all_to_all(images, 'sec', split_axis=2, concat_axis=1, tiled=True)]
    gather x2 -> x0, local copies, waits for them, and re-layouts: 7.83 us -> none  [the longest x1 4.64 us: shards(): jnp.take(regrouped[group], pair_src[group], axis=0).astype(jnp.float32)]
    all_to_all x3 -> x0, local copies, waits for them, and re-layouts: 6.71 us -> none  [the longest x2 3.9 us: shards(): lax.all_to_all(window_part, 'sec', split_axis=0, concat_axis=1, tiled=True)]
  transfers between devices with their start and end apart: 2 -> 0, of which waited for: 2 -> 0; matrix products, arithmetic and copies ran while one was open for 0% -> 0% of each run, Pallas kernels for 0% -> 0%
where the time goes in v1:
time: 108 us
  Pallas kernels  104 us (96%)
  other arithmetic  2.87 us (3%)
    pallas_call x1, Pallas kernels, shards(): pl.pallas_call(kernel, out_shape=jax.ShapeDtypeStruct((SECTORS_HERE, X_PA...  104 us

profile of v1, /device:TPU:1, one launch (start us, length us, event | category | flops | bytes accessed | tf_op | source)
XLA Modules:
  0.0 108.0 jit_solution(8785485352259554035)
XLA Ops:
  0.0 0.7 compare_select_fusion.2
  0.7 0.6 pad.4.slot_in
  1.3 0.0 copy-start
  1.3 104.5 %shard_map.55 = f32[8,48,384]{2,1,0:T(8,128)} custom-call(s32[8,256]{1,0:T(8,128)} %pad.4.slot_in, s32[2,8]{1,0:T(2,128)} %widths.1, bf16[8,384,384]{2,1,0:T(8,128)(2,1)} %psi.1, bf16[2,8,384,384]{3,2,1,0:T(8,128)(2,1)} %left.1, bf16[2,8,384,384]{3,2,1,0:T(8,128)(2,1)} %right.1), custom_call_target="tpu_custom_call" | custom-call | flops 3623878656 | bytes 11796480 | tf_op jit(solution)/shard_map/pallas_call | solution.py:317
  105.8 0.0 copy-done
  105.9 0.1 broadcast_compare_fusion
  105.9 0.1 iota_compare_fusion
  106.0 2.0 %bitcast_select_fusion = f32[8,384,48]{1,2,0:T(8,128)} fusion(f32[8,48,384]{2,1,0:T(8,128)} %shard_map.55, pred[8,48]{1,0:T(8,128)(4,1)S(1)} %broadcast_compare_fusion, pred[8,384]{1,0:T(8,128)(4,1)S(1)} %iota_compare_fusion), kind=kLoop, calls=%fused_computation | loop fusion | flops 294912 | bytes 1183104 | tf_op jit(solution)/shard_map/jit(_where)/select_n | solution.py:343
  (2 shorter events, 0.0 us)
Async XLA Ops:
  1.3 104.5 %copy-start = (s32[2,8]{1,0:T(2,128)S(1)}, s32[2,8]{1,0:T(2,128)}, u32[]{:S(2)}) copy-start(s32[2,8]{1,0:T(2,128)} %widths.1) | copy-start | bytes 196

commit v2 on v0

v2 whole, which is shorter than its diff:
```python
import jax
import jax.numpy as jnp
from jax import lax
from jax.experimental import pallas as pl
from jax.experimental.pallas import tpu as pltpu
from jax.sharding import PartitionSpec as P

NX, NY, NZ, NC = 4, 4, 8, 2
CHUNKS = 3
PIECES = ((0, 0, 3), (1, 0, 3), (2, 0, 2), (2, 2, 1))
SLOTS = NX * NY
GROUPS_HERE = 2
SECTORS_HERE = 8
TILE = GROUPS_HERE * SECTORS_HERE
SOURCES = SLOTS * TILE
X_PART = NX // NC
STEPS = NZ // 2
MESH = pl.DeviceIdType.MESH
BUFFERS = 11


def routes(sign):
    direct, relayed = [], []
    for dx in range(NX):
        for dy in range(NY):
            far_x, far_y = NX > 2 and dx == NX // 2, NY > 2 and dy == NY // 2
            if far_x or far_y:
                via = (sign if far_x else 0, sign if far_y else 0)
                relayed.append(((dx, dy), via, (dx - via[0], dy - via[1])))
            elif (dx, dy) != (0, 0):
                direct.append((dx, dy))
    return direct, relayed


RELAYS = len(routes(1)[1])


def device(x, y, z, c):
    return (x * NZ + z, y * NC + c)


def ones_where(condition):
    return jnp.where(condition, 1.0, 0.0).astype(jnp.bfloat16)


def tile_at(index):
    return pl.ds(pl.multiple_of(index * TILE, TILE), TILE)


def kernel(pair_src, widths, psi, left, right, out, *rest):
    psi_v, left_v, right_v, orders_own, orders, image, swap, pick, *rest = rest
    sends, rest = rest[:CHUNKS], rest[CHUNKS:]
    buffers = [rest[i * BUFFERS : (i + 1) * BUFFERS] for i in range(len(PIECES))]
    (
        load_sem, order_sem, order_send, spread_send, spread_recv, relay_recv, relay_send, core_send, core_recv,
        up_send, up_recv, down_send, down_recv, final_send, final_recv,
    ) = rest[len(PIECES) * BUFFERS :]
    got, relay, give, take, own, up_out, up_in, down_out, down_in, done, final = zip(*buffers)
    sec, term = lax.axis_index("sec"), lax.axis_index("term")
    x, z = lax.div(sec, NZ), lax.rem(sec, NZ)
    y, c = lax.div(term, NC), lax.rem(term, NC)
    size = psi_v.shape[-1]
    rows = size // SLOTS
    lanes = size // CHUNKS
    targets = pair_src.shape[1]
    pieces = range(len(PIECES))
    first_row = [rows * at // 3 for _, at, _ in PIECES]
    piece_rows = [rows * count // 3 for _, _, count in PIECES]

    def shifted(value, by, count):
        return lax.rem(value + (by % count), count)

    barrier = pltpu.get_barrier_semaphore()
    others = [
        device(shifted(x, dx, NX), shifted(y, dy, NY), z, c)
        for dx in range(NX)
        for dy in range(NY)
        if (dx, dy) != (0, 0)
    ]
    others += [device(shifted(x, dx, NX), y, z, 1 - c) for dx in range(NX)]
    others += [device(x, y, shifted(z, 1, NZ), c), device(x, y, shifted(z, -1, NZ), c)]
    for other in others:
        pl.semaphore_signal(barrier, inc=1, device_id=other, device_id_type=MESH)

    def loads(k):
        return (
            pltpu.make_async_copy(psi.at[k], psi_v.at[k], load_sem.at[0, k]),
            pltpu.make_async_copy(left.at[:, k], left_v.at[:, k], load_sem.at[1, k]),
            pltpu.make_async_copy(right.at[:, k], right_v.at[:, k], load_sem.at[2, k]),
        )

    for k in range(SECTORS_HERE):
        for copy in loads(k):
            copy.start()

    row = lax.broadcasted_iota(jnp.int32, swap.shape, 0)
    column = lax.broadcasted_iota(jnp.int32, swap.shape, 1)
    swap[...] = ones_where(row == (column & (TILE - 1)) * TILE + lax.shift_right_logical(column, 4))
    orders_own[...] = jnp.concatenate([pair_src[...], jnp.zeros((6, targets), jnp.int32)], 0)

    def images(chunk):
        def one(k, _):
            if chunk == 0:
                for copy in loads(k)[:2]:
                    copy.wait()
                keep = (lax.broadcasted_iota(jnp.int32, (size, size), 0) < widths[0, k]) & (
                    lax.broadcasted_iota(jnp.int32, (size, size), 1) < widths[1, k]
                )
                psi_v[k] = jnp.where(keep, psi_v[k].astype(jnp.float32), 0.0).astype(jnp.bfloat16)
            here = left_v[:, k, chunk * lanes : (chunk + 1) * lanes, :].reshape(2 * lanes, size)
            part = jnp.dot(here, psi_v[k], preferred_element_type=jnp.float32).astype(jnp.bfloat16)
            if chunk == 0:
                loads(k)[2].wait()
            for group in range(GROUPS_HERE):
                image[group * SECTORS_HERE + k] = lax.dot_general(
                    right_v[group, k],
                    part[group * lanes : (group + 1) * lanes],
                    (((1,), (1,)), ((), ())),
                    preferred_element_type=jnp.float32,
                ).astype(jnp.bfloat16)
            return 0

        lax.fori_loop(0, SECTORS_HERE, one, 0)

        def turn(step, _):
            for inner in range(2):
                low = step * (4 * TILE) + inner * (2 * TILE)
                both = [
                    image[:, pl.ds(pl.multiple_of(low + part * TILE, TILE), TILE), :].reshape(
                        TILE * TILE, lanes
                    )
                    for part in range(2)
                ]
                turned = jnp.dot(
                    swap[...], jnp.concatenate(both, 1), preferred_element_type=jnp.float32
                ).astype(jnp.bfloat16)
                for part in range(2):
                    sends[chunk][pl.ds(low + part * TILE, TILE)] = turned[
                        :, part * lanes : (part + 1) * lanes
                    ].reshape(TILE, TILE, lanes)
            return 0

        lax.fori_loop(0, size // (4 * TILE), turn, 0)

    def halves(piece):
        count = piece_rows[piece] // 2
        return ((0, 1, 0, count), (1, -1, count, count))

    def block_for(piece, x_to, y_to, low, count):
        start = (y_to * NX + x_to) * rows + first_row[piece] + low
        return sends[PIECES[piece][0]].at[pl.ds(start, count)]

    def place(piece, x_from, y_from, low, count):
        return got[piece].at[low : low + count, tile_at(y_from * NX + x_from)]

    def spread(piece):
        for half, sign, low, count in halves(piece):
            for j, ((dx, dy), (vx, vy), _) in enumerate(routes(sign)[1]):
                pltpu.make_async_remote_copy(
                    src_ref=block_for(piece, shifted(x, dx, NX), shifted(y, dy, NY), low, count),
                    dst_ref=relay[piece].at[half, j],
                    send_sem=spread_send.at[piece],
                    recv_sem=relay_recv.at[piece, half],
                    device_id=device(shifted(x, vx, NX), shifted(y, vy, NY), z, c),
                    device_id_type=MESH,
                ).start()
        count = piece_rows[piece]
        for dx, dy in routes(1)[0]:
            xd, yd = shifted(x, dx, NX), shifted(y, dy, NY)
            pltpu.make_async_remote_copy(
                src_ref=block_for(piece, xd, yd, 0, count),
                dst_ref=place(piece, x, y, 0, count),
                send_sem=spread_send.at[piece],
                recv_sem=spread_recv.at[piece],
                device_id=device(xd, yd, z, c),
                device_id_type=MESH,
            ).start()
        pltpu.make_async_copy(
            block_for(piece, x, y, 0, count), place(piece, x, y, 0, count), spread_recv.at[piece]
        ).start()

    def forward(piece):
        if RELAYS == 0:
            return
        for half, sign, low, count in halves(piece):
            arrived = relay[piece].at[half]
            pltpu.make_async_copy(arrived, arrived, relay_recv.at[piece, half]).wait()
            for j, (_, (vx, vy), (fx, fy)) in enumerate(routes(sign)[1]):
                pltpu.make_async_remote_copy(
                    src_ref=relay[piece].at[half, j],
                    dst_ref=place(piece, shifted(x, -vx, NX), shifted(y, -vy, NY), low, count),
                    send_sem=relay_send.at[piece],
                    recv_sem=spread_recv.at[piece],
                    device_id=device(shifted(x, fx, NX), shifted(y, fy, NY), z, c),
                    device_id_type=MESH,
                ).start()

    def order_copy(dy):
        return pltpu.make_async_remote_copy(
            src_ref=orders_own,
            dst_ref=orders.at[y],
            send_sem=order_send.at[dy],
            recv_sem=order_sem.at[0],
            device_id=device(x, shifted(y, dy, NY), z, c),
            device_id_type=MESH,
        )

    def make_pick():
        pltpu.make_async_copy(orders, orders, order_sem.at[0]).wait()
        line = lax.broadcasted_iota(jnp.int32, (SECTORS_HERE, targets), 0)
        blocks = []
        for yy in range(NY):
            for xx in range(NX):
                for group in range(GROUPS_HERE):
                    wanted = orders[yy, group : group + 1, :]
                    first = (xx * NZ + z) * SECTORS_HERE
                    blocks.append(jnp.where(wanted == line + first, 1.0, 0.0))
        table = jnp.concatenate(blocks, 0).T
        blocks = []
        for xh in range(NC):
            for zz in range(NZ):
                for part in range(X_PART):
                    low = ((xh * X_PART + part) * NZ + zz) * SECTORS_HERE
                    blocks.append(table[low : low + SECTORS_HERE])
        pick[...] = jnp.concatenate(blocks, 0).astype(jnp.bfloat16)

    def gather(piece, part, to):
        half = targets // NC
        chosen = pick[pl.ds(pl.multiple_of(part * half, half), half), :]

        def some(step, _):
            for inner in range(2):
                m = step * 4 + inner * 2
                both = jnp.concatenate([got[piece][m], got[piece][m + 1]], 1)
                value = jnp.dot(chosen, both, preferred_element_type=jnp.float32).astype(to.dtype)
                for zz in range(NZ):
                    for next_m in range(2):
                        to[zz, m + next_m] = value[
                            zz * TILE : (zz + 1) * TILE, next_m * lanes : (next_m + 1) * lanes
                        ]
            return 0

        lax.fori_loop(0, piece_rows[piece] // 4, some, 0)

    def core_copy(piece):
        return pltpu.make_async_remote_copy(
            src_ref=give[piece],
            dst_ref=take[piece],
            send_sem=core_send.at[piece],
            recv_sem=core_recv.at[piece],
            device_id=device(x, y, z, 1 - c),
            device_id_type=MESH,
        )

    def give_half(piece):
        pltpu.make_async_copy(got[piece], got[piece], spread_recv.at[piece]).wait()
        gather(piece, 1 - c, give[piece])
        core_copy(piece).start()

    def keep_half(piece):
        gather(piece, c, own[piece])

    def held(piece, zd, low, count):
        at = slice(low, low + count)
        return own[piece][zd, at] + take[piece][zd, at].astype(jnp.float32)

    def z_buffers(piece, way):
        return (up_out[piece], up_in[piece]) if way > 0 else (down_out[piece], down_in[piece])

    def z_copy(piece, step, way):
        source, target = z_buffers(piece, way)
        out_sem, in_sem = (up_send, up_recv) if way > 0 else (down_send, down_recv)
        at = (step,)
        if step == 0:
            _, _, low, count = halves(piece)[0 if way > 0 else 1]
            at = (step, slice(low, low + count))
        return pltpu.make_async_remote_copy(
            src_ref=source.at[at],
            dst_ref=target.at[at],
            send_sem=out_sem.at[piece, step],
            recv_sem=in_sem.at[piece, step],
            device_id=device(x, y, shifted(z, way, NZ), c),
            device_id_type=MESH,
        )

    def carried(step, way, sign):
        return step > 0 or way == sign

    def chain(piece, step):
        if step >= STEPS:
            return
        if step == 0:
            core_copy(piece).wait_recv()
        for way in (1, -1):
            source, target = z_buffers(piece, way)
            if step > 0:
                z_copy(piece, step - 1, way).wait_recv()
            zd = shifted(z, way * (STEPS - step), NZ)
            for _, sign, low, count in halves(piece):
                if carried(step, way, sign):
                    at = slice(low, low + count)
                    value = held(piece, zd, low, count)
                    if step > 0 and carried(step - 1, way, sign):
                        value = value + target[step - 1, at].astype(jnp.float32)
                    source[step, at] = value.astype(jnp.bfloat16)
            z_copy(piece, step, way).start()

    def final_copies(piece, part):
        xd = c * X_PART + part
        spot_there = final[piece].at[lax.rem(x, X_PART)]
        there = dict(
            src_ref=done[piece].at[part],
            dst_ref=spot_there,
            send_sem=final_send.at[piece, part],
            recv_sem=final_recv.at[piece],
            device_id=device(xd, y, z, lax.div(x, X_PART)),
            device_id_type=MESH,
        )
        here = (done[piece].at[part], spot_there, final_recv.at[piece])
        return xd, there, here

    def finish(piece):
        last = STEPS - 1
        for way in (1, -1):
            z_copy(piece, last, way).wait_recv()
        for _, sign, low, count in halves(piece):
            value = held(piece, z, low, count)
            for way in (1, -1):
                if carried(last, way, sign):
                    value = value + z_buffers(piece, way)[1][last, low : low + count].astype(jnp.float32)
            for part in range(X_PART):
                at = slice(part * SECTORS_HERE, (part + 1) * SECTORS_HERE)
                done[piece][part, low // 2 : (low + count) // 2] = (
                    value[:, at, :].reshape(count // 2, TILE, lanes).astype(jnp.bfloat16)
                )
        for part in range(X_PART):
            xd, there, here = final_copies(piece, part)

            @pl.when(xd != x)
            def _():
                pltpu.make_async_remote_copy(**there).start()

            @pl.when(xd == x)
            def _():
                pltpu.make_async_copy(*here).start()

    def put(piece):
        pltpu.make_async_copy(final[piece], final[piece], final_recv.at[piece]).wait()
        chunk, count = PIECES[piece][0], piece_rows[piece]
        total = X_PART * count * SECTORS_HERE
        row = lax.broadcasted_iota(jnp.int32, (total, total), 0)
        column = lax.broadcasted_iota(jnp.int32, (total, total), 1)
        sector = column & (SECTORS_HERE - 1)
        line = lax.shift_right_logical(column, 3)
        value = jnp.dot(
            ones_where(row == sector * (X_PART * count) + line),
            final[piece][...].reshape(total, lanes),
            preferred_element_type=jnp.float32,
        )
        for sector in range(SECTORS_HERE):
            for part in range(X_PART):
                low = part * rows + first_row[piece]
                start = (sector * X_PART + part) * count
                out[sector, low : low + count, chunk * lanes : (chunk + 1) * lanes] = value[
                    start : start + count
                ]

    images(0)
    pl.semaphore_wait(barrier, len(others))
    spread(0)
    for dy in range(1, NY):
        order_copy(dy).start()
    pltpu.make_async_copy(orders_own, orders.at[y], order_sem.at[0]).start()
    images(1)
    forward(0)
    spread(1)
    make_pick()
    images(2)
    give_half(0)
    keep_half(0)
    chain(0, 0)
    forward(1)
    spread(2)
    chain(0, 1)
    chain(0, 2)
    spread(3)
    chain(0, 3)
    finish(0)
    give_half(1)
    keep_half(1)
    chain(1, 0)
    forward(2)
    put(0)
    chain(1, 1)
    forward(3)
    chain(1, 2)
    chain(1, 3)
    finish(1)
    give_half(2)
    keep_half(2)
    chain(2, 0)
    give_half(3)
    chain(2, 1)
    keep_half(3)
    chain(3, 0)
    put(1)
    chain(2, 2)
    chain(3, 1)
    chain(2, 3)
    chain(3, 2)
    finish(2)
    chain(3, 3)
    put(2)
    finish(3)
    put(3)

    for dy in range(1, NY):
        order_copy(dy).wait_send()
    for piece in pieces:
        sent = sends[PIECES[piece][0]].at[0 : (SLOTS - 1) * piece_rows[piece]]
        pltpu.make_async_copy(sent, sent, spread_send.at[piece]).wait()
        if RELAYS:
            pltpu.make_async_copy(relay[piece], relay[piece], relay_send.at[piece]).wait()
        core_copy(piece).wait_send()
        for step in range(STEPS):
            for way in (1, -1):
                z_copy(piece, step, way).wait_send()
        for part in range(X_PART):
            xd, there, _ = final_copies(piece, part)

            @pl.when(xd != x)
            def _():
                pltpu.make_async_remote_copy(**there).wait_send()


def shards(psi, left_ops, right_ops, pair_src, widths):
    size = psi.shape[1]
    targets = pair_src.shape[1]
    rows, lanes = size // SLOTS, size // CHUNKS
    term = lax.axis_index("term")
    bf, count = jnp.bfloat16, len(PIECES)
    tile = (TILE, lanes)
    scratch = [
        pltpu.VMEM(psi.shape, bf),
        pltpu.VMEM(left_ops.shape, bf),
        pltpu.VMEM(right_ops.shape, bf),
        pltpu.VMEM((8, targets), jnp.int32),
        pltpu.VMEM((NY, 8, targets), jnp.int32),
        pltpu.VMEM((TILE, size, lanes), bf),
        pltpu.VMEM((TILE * TILE, TILE * TILE), bf),
        pltpu.VMEM((targets, SOURCES), bf),
        *[pltpu.VMEM((size,) + tile, bf) for _ in range(CHUNKS)],
    ]
    for _, _, thirds in PIECES:
        here = rows * thirds // 3
        ring = pltpu.VMEM((STEPS, here) + tile, bf)
        scratch += [
            pltpu.VMEM((here, SOURCES, lanes), bf),
            pltpu.VMEM((2, max(RELAYS, 1), here // 2) + tile, bf),
            pltpu.VMEM((NZ, here) + tile, bf),
            pltpu.VMEM((NZ, here) + tile, bf),
            pltpu.VMEM((NZ, here) + tile, jnp.float32),
            ring, ring, ring, ring,
            pltpu.VMEM((X_PART, here // 2) + tile, bf),
            pltpu.VMEM((X_PART, here // 2) + tile, bf),
        ]
    dma = pltpu.SemaphoreType.DMA
    scratch += [
        dma((3, SECTORS_HERE)), dma((1,)), dma((NY,)), dma((count,)), dma((count,)),
        dma((count, 2)), dma((count,)), dma((count,)), dma((count,)),
        dma((count, STEPS)), dma((count, STEPS)), dma((count, STEPS)), dma((count, STEPS)),
        dma((count, X_PART)), dma((count,)),
    ]
    summed = pl.pallas_call(
        kernel,
        out_shape=jax.ShapeDtypeStruct((SECTORS_HERE, X_PART * rows, size), jnp.float32),
        in_specs=[
            pl.BlockSpec(memory_space=pltpu.VMEM),
            pl.BlockSpec(memory_space=pltpu.SMEM),
            pl.BlockSpec(memory_space=pl.ANY),
            pl.BlockSpec(memory_space=pl.ANY),
            pl.BlockSpec(memory_space=pl.ANY),
        ],
        out_specs=pl.BlockSpec(memory_space=pltpu.VMEM),
        scratch_shapes=scratch,
        compiler_params=pltpu.CompilerParams(
            collective_id=0, has_side_effects=True, vmem_limit_bytes=56 * 1024 * 1024
        ),
        cost_estimate=pl.CostEstimate(
            flops=64 * size**3, bytes_accessed=40 * size * size * 2, transcendentals=0
        ),
    )(pair_src, widths, psi, left_ops, right_ops)

    summed = jnp.swapaxes(summed, 1, 2)
    line = jnp.arange(size, dtype=jnp.int32)
    columns = term * (X_PART * rows) + jnp.arange(X_PART * rows, dtype=jnp.int32)
    keep = (line[None, :, None] < widths[0][:, None, None]) & (
        columns[None, None, :] < widths[1][:, None, None]
    )
    return jnp.where(keep, summed, jnp.zeros_like(summed))


def solution(mesh):
    return jax.shard_map(
        shards,
        mesh=mesh,
        in_specs=(
            P("sec", None, None),
            P("term", "sec", None, None),
            P("term", "sec", None, None),
            P("term", None),
            P(None, "sec"),
        ),
        out_specs=P("sec", None, "term"),
        check_vma=False,
    )
```

time: 298 us -> 109 us (0.37)
  waiting for transfers between devices: 138 us -> 0 us
  Pallas kernels: 0 us -> 106 us
  blocking collectives: 80.5 us -> 0 us
  local copies, waits for them, and re-layouts: 28.6 us -> 0.76 us
  matrix products: 15 us -> 0 us
  between operations: 13.5 us -> 0.01 us
  starting transfers between devices: 12.3 us -> 0 us
  other arithmetic: 7.06 us -> 2.16 us
    pallas_call x0 -> x1, Pallas kernels: none -> 106 us  [shards(): pl.pallas_call(kernel, out_shape=jax.ShapeDtypeStruct((SECTORS_HERE, X_PA...]
    all_to_all x1 -> x0, waiting for transfers between devices: 103 us -> none  [shards(): lax.all_to_all(images, 'sec', split_axis=2, concat_axis=1, tiled=True)]
    all_to_all x1 -> x0, blocking collectives: 80.5 us -> none  [shards(): lax.all_to_all(window_part, 'sec', split_axis=0, concat_axis=1, tiled=True)]
    reduce_scatter x1 -> x0, waiting for transfers between devices: 35.1 us -> none  [shards(): lax.psum_scatter(returned.astype(jnp.float32).astype(jnp.bfloat16), 'term...]
    dot_general x2 -> x0, matrix products: 15 us -> none  [contract(): jnp.einsum('kil,kml->kim', half, right_block, preferred_element_type=jnp....]
    all_to_all x1 -> x0, starting transfers between devices: 12.1 us -> none  [shards(): lax.all_to_all(images, 'sec', split_axis=2, concat_axis=1, tiled=True)]
    gather x2 -> x0, local copies, waits for them, and re-layouts: 7.83 us -> none  [the longest x1 4.64 us: shards(): jnp.take(regrouped[group], pair_src[group], axis=0).astype(jnp.float32)]
    all_to_all x3 -> x0, local copies, waits for them, and re-layouts: 6.71 us -> none  [the longest x2 3.9 us: shards(): lax.all_to_all(window_part, 'sec', split_axis=0, concat_axis=1, tiled=True)]
  transfers between devices with their start and end apart: 2 -> 0, of which waited for: 2 -> 0; matrix products, arithmetic and copies ran while one was open for 0% -> 0% of each run, Pallas kernels for 0% -> 0%
where the time goes in v2:
time: 109 us
  Pallas kernels  106 us (97%)
  other arithmetic  2.16 us (2%)
    pallas_call x1, Pallas kernels, shards(): pl.pallas_call(kernel, out_shape=jax.ShapeDtypeStruct((SECTORS_HERE, X_PA...  106 us

profile of v2, /device:TPU:1, one launch (start us, length us, event | category | flops | bytes accessed | tf_op | source)
XLA Modules:
  0.0 108.7 jit_solution(5243866347436961367)
XLA Ops:
  0.0 0.8 slice_bitcast_fusion.1
  0.8 0.1 broadcast_compare_fusion
  0.8 0.1 iota_compare_fusion
  0.9 105.8 %shard_map.55 = f32[8,48,384]{2,1,0:T(8,128)} custom-call(s32[2,256]{1,0:T(2,128)} %pair_src.1, s32[2,8]{1,0:T(2,128)} %widths.1, bf16[8,384,384]{2,1,0:T(8,128)(2,1)} %psi.1, bf16[2,8,384,384]{3,2,1,0:T(8,128)(2,1)} %left.1, bf16[2,8,384,384]{3,2,1,0:T(8,128)(2,1)} %right.1), custom_call_target="tpu_custom_call" | custom-call | flops 3623878656 | bytes 11796480 | tf_op jit(solution)/shard_map/pallas_call | solution.py:474
  106.7 2.0 %bitcast_select_fusion = f32[8,384,48]{1,2,0:T(8,128)} fusion(f32[8,48,384]{2,1,0:T(8,128)} %shard_map.55, pred[8,48]{1,0:T(8,128)(4,1)S(1)} %broadcast_compare_fusion, pred[8,384]{1,0:T(8,128)(4,1)S(1)} %iota_compare_fusion), kind=kLoop, calls=%fused_computation | loop fusion | flops 294912 | bytes 1183104 | tf_op jit(solution)/shard_map/jit(_where)/select_n | solution.py:500
  (1 shorter events, 0.0 us)

commit v3 on v2

--- a/solution.py
+++ b/solution.py
@@ -48,7 +48,7 @@
 
 
 def kernel(pair_src, widths, psi, left, right, out, *rest):
-    psi_v, left_v, right_v, orders_own, orders, image, swap, pick, *rest = rest
+    psi_v, left_v, right_v, orders_own, orders, parts, image, swap, pick, *rest = rest
     sends, rest = rest[:CHUNKS], rest[CHUNKS:]
     buffers = [rest[i * BUFFERS : (i + 1) * BUFFERS] for i in range(len(PIECES))]
     (
@@ -64,6 +64,7 @@
     lanes = size // CHUNKS
     targets = pair_src.shape[1]
     pieces = range(len(PIECES))
+    y_order = sorted(range(NY), key=lambda dy: -min(dy, NY - dy))
     first_row = [rows * at // 3 for _, at, _ in PIECES]
     piece_rows = [rows * count // 3 for _, _, count in PIECES]
 
@@ -89,58 +90,86 @@
             pltpu.make_async_copy(right.at[:, k], right_v.at[:, k], load_sem.at[2, k]),
         )
 
-    for k in range(SECTORS_HERE):
-        for copy in loads(k):
-            copy.start()
+    for which in ((0, 1), (2,)):
+        for k in range(SECTORS_HERE):
+            for copy in which:
+                loads(k)[copy].start()
 
     row = lax.broadcasted_iota(jnp.int32, swap.shape, 0)
     column = lax.broadcasted_iota(jnp.int32, swap.shape, 1)
     swap[...] = ones_where(row == (column & (TILE - 1)) * TILE + lax.shift_right_logical(column, 4))
     orders_own[...] = jnp.concatenate([pair_src[...], jnp.zeros((6, targets), jnp.int32)], 0)
 
+    def part_of(k, chunk):
+        here = left_v[:, k, chunk * lanes : (chunk + 1) * lanes, :].reshape(2 * lanes, size)
+        return jnp.dot(here, psi_v[k], preferred_element_type=jnp.float32).astype(jnp.bfloat16)
+
+    def image_of(k, group, at, part):
+        return lax.dot_general(
+            right_v[group, k, at, :], part, (((1,), (1,)), ((), ())), preferred_element_type=jnp.float32
+        ).astype(jnp.bfloat16)
+
+    def turn(chunk, low, start):
+        both = [
+            image[:, pl.ds(pl.multiple_of(low + part * TILE, TILE), TILE), :].reshape(TILE * TILE, lanes)
+            for part in range(2)
+        ]
+        turned = jnp.dot(
+            swap[...], jnp.concatenate(both, 1), preferred_element_type=jnp.float32
+        ).astype(jnp.bfloat16)
+        for part in range(2):
+            sends[chunk][pl.ds(start + part * TILE, TILE)] = turned[
+                :, part * lanes : (part + 1) * lanes
+            ].reshape(TILE, TILE, lanes)
+
+    def first_parts():
+        def one(k, _):
+            for copy in loads(k)[:2]:
+                copy.wait()
+            keep = (lax.broadcasted_iota(jnp.int32, (size, size), 0) < widths[0, k]) & (
+                lax.broadcasted_iota(jnp.int32, (size, size), 1) < widths[1, k]
+            )
+            psi_v[k] = jnp.where(keep, psi_v[k].astype(jnp.float32), 0.0).astype(jnp.bfloat16)
+            parts[k] = part_of(k, 0)
+            return 0
+
+        lax.fori_loop(0, SECTORS_HERE, one, 0)
+
+    def first_images(dy):
+        count = size // NY
+        start = shifted(y, dy, NY) * count
+        at = pl.ds(pl.multiple_of(start, 2 * TILE), count)
+
+        def one(k, _):
+            if dy == y_order[0]:
+                loads(k)[2].wait()
+            for group in range(GROUPS_HERE):
+                part = parts[k, group * lanes : (group + 1) * lanes, :]
+                image[group * SECTORS_HERE + k, 0:count, :] = image_of(k, group, at, part)
+            return 0
+
+        lax.fori_loop(0, SECTORS_HERE, one, 0)
+        for low in range(0, count, 2 * TILE):
+            turn(0, low, start + low)
+
     def images(chunk):
         def one(k, _):
-            if chunk == 0:
-                for copy in loads(k)[:2]:
-                    copy.wait()
-                keep = (lax.broadcasted_iota(jnp.int32, (size, size), 0) < widths[0, k]) & (
-                    lax.broadcasted_iota(jnp.int32, (size, size), 1) < widths[1, k]
+            part = part_of(k, chunk)
+            for group in range(GROUPS_HERE):
+                image[group * SECTORS_HERE + k] = image_of(
+                    k, group, slice(None), part[group * lanes : (group + 1) * lanes]
                 )
-                psi_v[k] = jnp.where(keep, psi_v[k].astype(jnp.float32), 0.0).astype(jnp.bfloat16)
-            here = left_v[:, k, chunk * lanes : (chunk + 1) * lanes, :].reshape(2 * lanes, size)
-            part = jnp.dot(here, psi_v[k], preferred_element_type=jnp.float32).astype(jnp.bfloat16)
-            if chunk == 0:
-                loads(k)[2].wait()
-            for group in range(GROUPS_HERE):
-                image[group * SECTORS_HERE + k] = lax.dot_general(
-                    right_v[group, k],
-                    part[group * lanes : (group + 1) * lanes],
-                    (((1,), (1,)), ((), ())),
-                    preferred_element_type=jnp.float32,
-                ).astype(jnp.bfloat16)
             return 0
 
         lax.fori_loop(0, SECTORS_HERE, one, 0)
 
-        def turn(step, _):
+        def some(step, _):
             for inner in range(2):
                 low = step * (4 * TILE) + inner * (2 * TILE)
-                both = [
-                    image[:, pl.ds(pl.multiple_of(low + part * TILE, TILE), TILE), :].reshape(
-                        TILE * TILE, lanes
-                    )
-                    for part in range(2)
-                ]
-                turned = jnp.dot(
-                    swap[...], jnp.concatenate(both, 1), preferred_element_type=jnp.float32
-                ).astype(jnp.bfloat16)
-                for part in range(2):
-                    sends[chunk][pl.ds(low + part * TILE, TILE)] = turned[
-                        :, part * lanes : (part + 1) * lanes
-                    ].reshape(TILE, TILE, lanes)
+                turn(chunk, low, low)
             return 0
 
-        lax.fori_loop(0, size // (4 * TILE), turn, 0)
+        lax.fori_loop(0, size // (4 * TILE), some, 0)
 
     def halves(piece):
         count = piece_rows[piece] // 2
@@ -153,31 +182,34 @@
     def place(piece, x_from, y_from, low, count):
         return got[piece].at[low : low + count, tile_at(y_from * NX + x_from)]
 
-    def spread(piece):
+    def spread(piece, rings=range(NY)):
         for half, sign, low, count in halves(piece):
             for j, ((dx, dy), (vx, vy), _) in enumerate(routes(sign)[1]):
+                if dy in rings:
+                    pltpu.make_async_remote_copy(
+                        src_ref=block_for(piece, shifted(x, dx, NX), shifted(y, dy, NY), low, count),
+                        dst_ref=relay[piece].at[half, j],
+                        send_sem=spread_send.at[piece],
+                        recv_sem=relay_recv.at[piece, half],
+                        device_id=device(shifted(x, vx, NX), shifted(y, vy, NY), z, c),
+                        device_id_type=MESH,
+                    ).start()
+        count = piece_rows[piece]
+        for dx, dy in routes(1)[0]:
+            if dy in rings:
+                xd, yd = shifted(x, dx, NX), shifted(y, dy, NY)
                 pltpu.make_async_remote_copy(
-                    src_ref=block_for(piece, shifted(x, dx, NX), shifted(y, dy, NY), low, count),
-                    dst_ref=relay[piece].at[half, j],
+                    src_ref=block_for(piece, xd, yd, 0, count),
+                    dst_ref=place(piece, x, y, 0, count),
                     send_sem=spread_send.at[piece],
-                    recv_sem=relay_recv.at[piece, half],
-                    device_id=device(shifted(x, vx, NX), shifted(y, vy, NY), z, c),
+                    recv_sem=spread_recv.at[piece],
+                    device_id=device(xd, yd, z, c),
                     device_id_type=MESH,
                 ).start()
-        count = piece_rows[piece]
-        for dx, dy in routes(1)[0]:
-            xd, yd = shifted(x, dx, NX), shifted(y, dy, NY)
-            pltpu.make_async_remote_copy(
-                src_ref=block_for(piece, xd, yd, 0, count),
-                dst_ref=place(piece, x, y, 0, count),
-                send_sem=spread_send.at[piece],
-                recv_sem=spread_recv.at[piece],
-                device_id=device(xd, yd, z, c),
-                device_id_type=MESH,
+        if 0 in rings:
+            pltpu.make_async_copy(
+                block_for(piece, x, y, 0, count), place(piece, x, y, 0, count), spread_recv.at[piece]
             ).start()
-        pltpu.make_async_copy(
-            block_for(piece, x, y, 0, count), place(piece, x, y, 0, count), spread_recv.at[piece]
-        ).start()
 
     def forward(piece):
         if RELAYS == 0:
@@ -365,9 +397,12 @@
                     start : start + count
                 ]
 
-    images(0)
-    pl.semaphore_wait(barrier, len(others))
-    spread(0)
+    first_parts()
+    for dy in y_order:
+        first_images(dy)
+        if dy == y_order[0]:
+            pl.semaphore_wait(barrier, len(others))
+        spread(0, (dy,))
     for dy in range(1, NY):
         order_copy(dy).start()
     pltpu.make_async_copy(orders_own, orders.at[y], order_sem.at[0]).start()
@@ -378,40 +413,40 @@
     images(2)
     give_half(0)
     keep_half(0)
-    chain(0, 0)
     forward(1)
     spread(2)
+    chain(0, 0)
+    spread(3)
     chain(0, 1)
     chain(0, 2)
-    spread(3)
-    chain(0, 3)
-    finish(0)
     give_half(1)
     keep_half(1)
+    chain(0, 3)
+    forward(2)
     chain(1, 0)
-    forward(2)
-    put(0)
+    finish(0)
     chain(1, 1)
     forward(3)
+    put(0)
     chain(1, 2)
-    chain(1, 3)
-    finish(1)
     give_half(2)
     keep_half(2)
+    chain(1, 3)
     chain(2, 0)
     give_half(3)
-    chain(2, 1)
     keep_half(3)
     chain(3, 0)
+    finish(1)
+    chain(2, 1)
+    chain(3, 1)
     put(1)
     chain(2, 2)
-    chain(3, 1)
+    chain(3, 2)
     chain(2, 3)
-    chain(3, 2)
+    chain(3, 3)
     finish(2)
-    chain(3, 3)
+    finish(3)
     put(2)
-    finish(3)
     put(3)
 
     for dy in range(1, NY):
@@ -446,6 +481,7 @@
         pltpu.VMEM(right_ops.shape, bf),
         pltpu.VMEM((8, targets), jnp.int32),
         pltpu.VMEM((NY, 8, targets), jnp.int32),
+        pltpu.VMEM((SECTORS_HERE, 2 * lanes, size), bf),
         pltpu.VMEM((TILE, size, lanes), bf),
         pltpu.VMEM((TILE * TILE, TILE * TILE), bf),
         pltpu.VMEM((targets, SOURCES), bf),

time: 109 us -> 96.6 us (0.89)
  Pallas kernels: 106 us -> 93.5 us
    pallas_call x1, Pallas kernels: 106 us -> 93.5 us  [shards(): pl.pallas_call(kernel, out_shape=jax.ShapeDtypeStruct((SECTORS_HERE, X_PA...]
where the time goes in v3:
time: 96.6 us; the launch traced here: 96.5 us
  Pallas kernels  93.5 us (97%)
  other arithmetic  2.16 us (2%)
    pallas_call x1, Pallas kernels, shards(): pl.pallas_call(kernel, out_shape=jax.ShapeDtypeStruct((SECTORS_HERE, X_PA...  93.5 us
    select_n x1, other arithmetic, shards(): return jnp.where(keep, summed, jnp.zeros_like(summed))  2.01 us

profile of v3, /device:TPU:1, one launch (start us, length us, event | category | flops | bytes accessed | tf_op | source)
XLA Modules:
  0.0 96.5 jit_solution(17637314489582360822)
XLA Ops:
  0.0 0.8 slice_bitcast_fusion.1
  0.8 0.1 broadcast_compare_fusion
  0.8 0.1 iota_compare_fusion
  0.9 93.5 %shard_map.55 = f32[8,48,384]{2,1,0:T(8,128)} custom-call(s32[2,256]{1,0:T(2,128)} %pair_src.1, s32[2,8]{1,0:T(2,128)} %widths.1, bf16[8,384,384]{2,1,0:T(8,128)(2,1)} %psi.1, bf16[2,8,384,384]{3,2,1,0:T(8,128)(2,1)} %left.1, bf16[2,8,384,384]{3,2,1,0:T(8,128)(2,1)} %right.1), custom_call_target="tpu_custom_call" | custom-call | flops 3623878656 | bytes 11796480 | tf_op jit(solution)/shard_map/pallas_call | solution.py:510
  94.5 2.0 %bitcast_select_fusion = f32[8,384,48]{1,2,0:T(8,128)} fusion(f32[8,48,384]{2,1,0:T(8,128)} %shard_map.55, pred[8,48]{1,0:T(8,128)(4,1)S(1)} %broadcast_compare_fusion, pred[8,384]{1,0:T(8,128)(4,1)S(1)} %iota_compare_fusion), kind=kLoop, calls=%fused_computation | loop fusion | flops 294912 | bytes 1183104 | tf_op jit(solution)/shard_map/jit(_where)/select_n | solution.py:536
  (1 shorter events, 0.0 us)

commit v4 on v3

--- a/solution.py
+++ b/solution.py
@@ -100,73 +100,94 @@
     swap[...] = ones_where(row == (column & (TILE - 1)) * TILE + lax.shift_right_logical(column, 4))
     orders_own[...] = jnp.concatenate([pair_src[...], jnp.zeros((6, targets), jnp.int32)], 0)
 
-    def part_of(k, chunk):
-        here = left_v[:, k, chunk * lanes : (chunk + 1) * lanes, :].reshape(2 * lanes, size)
-        return jnp.dot(here, psi_v[k], preferred_element_type=jnp.float32).astype(jnp.bfloat16)
-
-    def image_of(k, group, at, part):
+    def image_of(right_block, part):
         return lax.dot_general(
-            right_v[group, k, at, :], part, (((1,), (1,)), ((), ())), preferred_element_type=jnp.float32
+            right_block, part, (((1,), (1,)), ((), ())), preferred_element_type=jnp.float32
         ).astype(jnp.bfloat16)
 
-    def turn(chunk, low, start):
-        both = [
-            image[:, pl.ds(pl.multiple_of(low + part * TILE, TILE), TILE), :].reshape(TILE * TILE, lanes)
-            for part in range(2)
-        ]
-        turned = jnp.dot(
-            swap[...], jnp.concatenate(both, 1), preferred_element_type=jnp.float32
-        ).astype(jnp.bfloat16)
-        for part in range(2):
-            sends[chunk][pl.ds(start + part * TILE, TILE)] = turned[
-                :, part * lanes : (part + 1) * lanes
-            ].reshape(TILE, TILE, lanes)
+    def turned(block):
+        return jnp.dot(swap[...], block, preferred_element_type=jnp.float32).astype(jnp.bfloat16)
+
+    def each_sector(body):
+        def some(step, _):
+            for inner in range(2):
+                body(step * 2 + inner)
+            return 0
+
+        lax.fori_loop(0, SECTORS_HERE // 2, some, 0)
 
     def first_parts():
-        def one(k, _):
+        def one(k):
             for copy in loads(k)[:2]:
                 copy.wait()
             keep = (lax.broadcasted_iota(jnp.int32, (size, size), 0) < widths[0, k]) & (
                 lax.broadcasted_iota(jnp.int32, (size, size), 1) < widths[1, k]
             )
-            psi_v[k] = jnp.where(keep, psi_v[k].astype(jnp.float32), 0.0).astype(jnp.bfloat16)
-            parts[k] = part_of(k, 0)
-            return 0
-
-        lax.fori_loop(0, SECTORS_HERE, one, 0)
-
-    def first_images(dy):
+            masked = jnp.where(keep, psi_v[k].astype(jnp.float32), 0.0).astype(jnp.bfloat16)
+            psi_v[k] = masked
+            here = left_v[:, k, 0:lanes, :].reshape(GROUPS_HERE * lanes, size)
+            parts[k, 0 : GROUPS_HERE * lanes] = jnp.dot(
+                here, masked, preferred_element_type=jnp.float32
+            ).astype(jnp.bfloat16)
+
+        each_sector(one)
+
+    def first_images(rings, first):
         count = size // NY
-        start = shifted(y, dy, NY) * count
-        at = pl.ds(pl.multiple_of(start, 2 * TILE), count)
-
-        def one(k, _):
-            if dy == y_order[0]:
+        starts = [pl.multiple_of(shifted(y, dy, NY) * count, 2 * TILE) for dy in rings]
+
+        def one(k):
+            if first:
                 loads(k)[2].wait()
             for group in range(GROUPS_HERE):
-                part = parts[k, group * lanes : (group + 1) * lanes, :]
-                image[group * SECTORS_HERE + k, 0:count, :] = image_of(k, group, at, part)
-            return 0
-
-        lax.fori_loop(0, SECTORS_HERE, one, 0)
-        for low in range(0, count, 2 * TILE):
-            turn(0, low, start + low)
-
-    def images(chunk):
-        def one(k, _):
-            part = part_of(k, chunk)
+                chosen = jnp.concatenate([right_v[group, k, pl.ds(start, count), :] for start in starts], 0)
+                image[group * SECTORS_HERE + k, 0 : count * len(starts), 0:lanes] = image_of(
+                    chosen, parts[k, group * lanes : (group + 1) * lanes, :]
+                )
+
+        each_sector(one)
+        for low in range(0, count * len(starts), 2 * TILE):
+            both = turned(
+                jnp.concatenate(
+                    [
+                        image[:, at : at + TILE, 0:lanes].reshape(TILE * TILE, lanes)
+                        for at in (low, low + TILE)
+                    ],
+                    1,
+                )
+            )
+            for part in range(2):
+                at = starts[low // count] + low % count + part * TILE
+                sends[0][pl.ds(at, TILE)] = both[:, part * lanes : (part + 1) * lanes].reshape(
+                    TILE, TILE, lanes
+                )
+
+    later = size - lanes
+
+    def later_parts():
+        def one(k):
+            here = left_v[:, k, lanes:, :].reshape(GROUPS_HERE * later, size)
+            parts[k] = jnp.dot(here, psi_v[k], preferred_element_type=jnp.float32).astype(jnp.bfloat16)
+
+        each_sector(one)
+
+    def later_images():
+        def one(k):
             for group in range(GROUPS_HERE):
                 image[group * SECTORS_HERE + k] = image_of(
-                    k, group, slice(None), part[group * lanes : (group + 1) * lanes]
+                    right_v[group, k], parts[k, group * later : (group + 1) * later, :]
                 )
-            return 0
-
-        lax.fori_loop(0, SECTORS_HERE, one, 0)
+
+        each_sector(one)
 
         def some(step, _):
-            for inner in range(2):
-                low = step * (4 * TILE) + inner * (2 * TILE)
-                turn(chunk, low, low)
+            for inner in range(4):
+                at = pl.multiple_of((step * 4 + inner) * TILE, TILE)
+                value = turned(image[:, pl.ds(at, TILE), :].reshape(TILE * TILE, later))
+                for chunk in range(1, CHUNKS):
+                    sends[chunk][pl.ds(at, TILE)] = value[
+                        :, (chunk - 1) * lanes : chunk * lanes
+                    ].reshape(TILE, TILE, lanes)
             return 0
 
         lax.fori_loop(0, size // (4 * TILE), some, 0)
@@ -248,31 +269,36 @@
                     first = (xx * NZ + z) * SECTORS_HERE
                     blocks.append(jnp.where(wanted == line + first, 1.0, 0.0))
         table = jnp.concatenate(blocks, 0).T
-        blocks = []
+        half = targets // NC
         for xh in range(NC):
+            blocks = []
             for zz in range(NZ):
                 for part in range(X_PART):
                     low = ((xh * X_PART + part) * NZ + zz) * SECTORS_HERE
                     blocks.append(table[low : low + SECTORS_HERE])
-        pick[...] = jnp.concatenate(blocks, 0).astype(jnp.bfloat16)
-
-    def gather(piece, part, to):
+            start = pl.multiple_of((1 - c if xh == 0 else c) * half, half)
+            pick[pl.ds(start, half), :] = jnp.concatenate(blocks, 0).astype(jnp.bfloat16)
+
+    def gather(piece):
+        pltpu.make_async_copy(got[piece], got[piece], spread_recv.at[piece]).wait()
         half = targets // NC
-        chosen = pick[pl.ds(pl.multiple_of(part * half, half), half), :]
 
         def some(step, _):
-            for inner in range(2):
-                m = step * 4 + inner * 2
+            for inner in range(4):
+                m = step * 8 + inner * 2
                 both = jnp.concatenate([got[piece][m], got[piece][m + 1]], 1)
-                value = jnp.dot(chosen, both, preferred_element_type=jnp.float32).astype(to.dtype)
-                for zz in range(NZ):
-                    for next_m in range(2):
-                        to[zz, m + next_m] = value[
-                            zz * TILE : (zz + 1) * TILE, next_m * lanes : (next_m + 1) * lanes
-                        ]
+                value = jnp.dot(pick[...], both, preferred_element_type=jnp.float32)
+                for part, to in ((0, give[piece]), (1, own[piece])):
+                    for zz in range(NZ):
+                        low = part * half + zz * TILE
+                        for next_m in range(2):
+                            to[zz, m + next_m] = value[
+                                low : low + TILE, next_m * lanes : (next_m + 1) * lanes
+                            ].astype(to.dtype)
             return 0
 
-        lax.fori_loop(0, piece_rows[piece] // 4, some, 0)
+        lax.fori_loop(0, piece_rows[piece] // 8, some, 0)
+        core_copy(piece).start()
 
     def core_copy(piece):
         return pltpu.make_async_remote_copy(
@@ -283,14 +309,6 @@
             device_id=device(x, y, z, 1 - c),
             device_id_type=MESH,
         )
-
-    def give_half(piece):
-        pltpu.make_async_copy(got[piece], got[piece], spread_recv.at[piece]).wait()
-        gather(piece, 1 - c, give[piece])
-        core_copy(piece).start()
-
-    def keep_half(piece):
-        gather(piece, c, own[piece])
 
     def held(piece, zd, low, count):
         at = slice(low, low + count)
@@ -398,29 +416,28 @@
                 ]
 
     first_parts()
-    for dy in y_order:
-        first_images(dy)
-        if dy == y_order[0]:
+    for part in range(2):
+        rings = y_order[part * NY // 2 : (part + 1) * NY // 2]
+        first_images(rings, part == 0)
+        if part == 0:
             pl.semaphore_wait(barrier, len(others))
-        spread(0, (dy,))
+        spread(0, rings)
     for dy in range(1, NY):
         order_copy(dy).start()
     pltpu.make_async_copy(orders_own, orders.at[y], order_sem.at[0]).start()
-    images(1)
+    later_parts()
     forward(0)
+    later_images()
     spread(1)
     make_pick()
-    images(2)
-    give_half(0)
-    keep_half(0)
+    gather(0)
     forward(1)
     spread(2)
     chain(0, 0)
     spread(3)
     chain(0, 1)
     chain(0, 2)
-    give_half(1)
-    keep_half(1)
+    gather(1)
     chain(0, 3)
     forward(2)
     chain(1, 0)
@@ -429,14 +446,12 @@
     forward(3)
     put(0)
     chain(1, 2)
-    give_half(2)
-    keep_half(2)
+    gather(2)
     chain(1, 3)
     chain(2, 0)
-    give_half(3)
-    keep_half(3)
+    gather(3)
+    finish(1)
     chain(3, 0)
-    finish(1)
     chain(2, 1)
     chain(3, 1)
     put(1)
@@ -481,8 +496,8 @@
         pltpu.VMEM(right_ops.shape, bf),
         pltpu.VMEM((8, targets), jnp.int32),
         pltpu.VMEM((NY, 8, targets), jnp.int32),
-        pltpu.VMEM((SECTORS_HERE, 2 * lanes, size), bf),
-        pltpu.VMEM((TILE, size, lanes), bf),
+        pltpu.VMEM((SECTORS_HERE, GROUPS_HERE * (size - lanes), size), bf),
+        pltpu.VMEM((TILE, size, size - lanes), bf),
         pltpu.VMEM((TILE * TILE, TILE * TILE), bf),
         pltpu.VMEM((targets, SOURCES), bf),
         *[pltpu.VMEM((size,) + tile, bf) for _ in range(CHUNKS)],

time: 96.6 us -> 96 us (level)
  no operation moved by 1% of the time
where the time goes in v4:
time: 96 us; the launch traced here: 95.8 us
  Pallas kernels  92.9 us (97%)
  other arithmetic  2.16 us (2%)
    pallas_call x1, Pallas kernels, shards(): pl.pallas_call(kernel, out_shape=jax.ShapeDtypeStruct((SECTORS_HERE, X_PA...  92.9 us
    select_n x1, other arithmetic, shards(): return jnp.where(keep, summed, jnp.zeros_like(summed))  2.01 us

profile of v4, /device:TPU:1, one launch (start us, length us, event | category | flops | bytes accessed | tf_op | source)
XLA Modules:
  0.0 95.8 jit_solution(10236189227913183267)
XLA Ops:
  0.0 0.8 slice_bitcast_fusion.1
  0.8 0.1 broadcast_compare_fusion
  0.8 0.1 iota_compare_fusion
  0.9 92.9 %shard_map.55 = f32[8,48,384]{2,1,0:T(8,128)} custom-call(s32[2,256]{1,0:T(2,128)} %pair_src.1, s32[2,8]{1,0:T(2,128)} %widths.1, bf16[8,384,384]{2,1,0:T(8,128)(2,1)} %psi.1, bf16[2,8,384,384]{3,2,1,0:T(8,128)(2,1)} %left.1, bf16[2,8,384,384]{3,2,1,0:T(8,128)(2,1)} %right.1), custom_call_target="tpu_custom_call" | custom-call | flops 3623878656 | bytes 11796480 | tf_op jit(solution)/shard_map/pallas_call | solution.py:525
  93.8 2.0 %bitcast_select_fusion = f32[8,384,48]{1,2,0:T(8,128)} fusion(f32[8,48,384]{2,1,0:T(8,128)} %shard_map.55, pred[8,48]{1,0:T(8,128)(4,1)S(1)} %broadcast_compare_fusion, pred[8,384]{1,0:T(8,128)(4,1)S(1)} %iota_compare_fusion), kind=kLoop, calls=%fused_computation | loop fusion | flops 294912 | bytes 1183104 | tf_op jit(solution)/shard_map/jit(_where)/select_n | solution.py:551
  (1 shorter events, 0.0 us)

commit v5 on v4

--- a/solution.py
+++ b/solution.py
@@ -16,19 +16,26 @@
 X_PART = NX // NC
 STEPS = NZ // 2
 MESH = pl.DeviceIdType.MESH
-BUFFERS = 11
+LANES = 128
+BUFFERS = 12
 
 
 def routes(sign):
     direct, relayed = [], []
-    for dx in range(NX):
-        for dy in range(NY):
-            far_x, far_y = NX > 2 and dx == NX // 2, NY > 2 and dy == NY // 2
-            if far_x or far_y:
-                via = (sign if far_x else 0, sign if far_y else 0)
-                relayed.append(((dx, dy), via, (dx - via[0], dy - via[1])))
-            elif (dx, dy) != (0, 0):
-                direct.append((dx, dy))
+    for dx, dy in sorted(
+        [(dx, dy) for dx in range(NX) for dy in range(NY)],
+        key=lambda move: (min(move[0], NX - move[0]) + min(move[1], NY - move[1]), move[0] == 0, move),
+    ):
+        far_x, far_y = NX > 2 and dx == NX // 2, NY > 2 and dy == NY // 2
+        if far_x or far_y:
+            via = (sign if far_x else 0, sign if far_y else 0)
+            relayed.append(((dx, dy), via, (dx - via[0], dy - via[1])))
+        elif (dx, dy) != (0, 0):
+            direct.append((dx, dy))
+    by_x = [route for route in relayed if route[1][0] != 0]
+    by_y = [route for route in relayed if route[1][0] == 0]
+    relayed = [route for pair in zip(by_x, by_y) for route in pair]
+    relayed += by_x[len(by_y) :] + by_y[len(by_x) :]
     return direct, relayed
 
 
@@ -55,7 +62,7 @@
         load_sem, order_sem, order_send, spread_send, spread_recv, relay_recv, relay_send, core_send, core_recv,
         up_send, up_recv, down_send, down_recv, final_send, final_recv,
     ) = rest[len(PIECES) * BUFFERS :]
-    got, relay, give, take, own, up_out, up_in, down_out, down_in, done, final = zip(*buffers)
+    got, relay, give, take, own, up_out, up_in, down_out, down_in, done, final, spots = zip(*buffers)
     sec, term = lax.axis_index("sec"), lax.axis_index("term")
     x, z = lax.div(sec, NZ), lax.rem(sec, NZ)
     y, c = lax.div(term, NC), lax.rem(term, NC)
@@ -204,8 +211,9 @@
         return got[piece].at[low : low + count, tile_at(y_from * NX + x_from)]
 
     def spread(piece, rings=range(NY)):
-        for half, sign, low, count in halves(piece):
-            for j, ((dx, dy), (vx, vy), _) in enumerate(routes(sign)[1]):
+        for j in range(RELAYS):
+            for half, sign, low, count in halves(piece):
+                (dx, dy), (vx, vy), _ = routes(sign)[1][j]
                 if dy in rings:
                     pltpu.make_async_remote_copy(
                         src_ref=block_for(piece, shifted(x, dx, NX), shifted(y, dy, NY), low, count),
@@ -235,10 +243,12 @@
     def forward(piece):
         if RELAYS == 0:
             return
-        for half, sign, low, count in halves(piece):
+        for half in range(2):
             arrived = relay[piece].at[half]
             pltpu.make_async_copy(arrived, arrived, relay_recv.at[piece, half]).wait()
-            for j, (_, (vx, vy), (fx, fy)) in enumerate(routes(sign)[1]):
+        for j in range(RELAYS):
+            for half, sign, low, count in halves(piece):
+                _, (vx, vy), (fx, fy) = routes(sign)[1][j]
                 pltpu.make_async_remote_copy(
                     src_ref=relay[piece].at[half, j],
                     dst_ref=place(piece, shifted(x, -vx, NX), shifted(y, -vy, NY), low, count),
@@ -394,26 +404,37 @@
             def _():
                 pltpu.make_async_copy(*here).start()
 
-    def put(piece):
-        pltpu.make_async_copy(final[piece], final[piece], final_recv.at[piece]).wait()
-        chunk, count = PIECES[piece][0], piece_rows[piece]
-        total = X_PART * count * SECTORS_HERE
-        row = lax.broadcasted_iota(jnp.int32, (total, total), 0)
-        column = lax.broadcasted_iota(jnp.int32, (total, total), 1)
-        sector = column & (SECTORS_HERE - 1)
-        line = lax.shift_right_logical(column, 3)
-        value = jnp.dot(
-            ones_where(row == sector * (X_PART * count) + line),
-            final[piece][...].reshape(total, lanes),
-            preferred_element_type=jnp.float32,
-        )
+    def make_spots():
+        for piece in pieces:
+            total, columns = spots[piece].shape
+            count = piece_rows[piece]
+            row = lax.broadcasted_iota(jnp.int32, (total, 1), 0)
+            line = lax.shift_right_logical(row, 3)
+            line = line + jnp.where(line < count, 0, rows - count) + first_row[piece]
+            spot = (row & (SECTORS_HERE - 1)) * LANES + line
+            spots[piece][...] = ones_where(
+                lax.broadcasted_iota(jnp.int32, (total, columns), 1) == spot
+            )
+
+    def put(chunk):
+        value = None
+        for piece in pieces:
+            if PIECES[piece][0] == chunk:
+                pltpu.make_async_copy(final[piece], final[piece], final_recv.at[piece]).wait()
+                here = lax.dot_general(
+                    final[piece][...].reshape(spots[piece].shape[0], lanes),
+                    spots[piece][...],
+                    (((0,), (0,)), ((), ())),
+                    preferred_element_type=jnp.float32,
+                )
+                value = here if value is None else value + here
+        width = X_PART * rows
+        row = chunk * lanes + lax.broadcasted_iota(jnp.int32, (lanes, width), 0)
+        column = term * width + lax.broadcasted_iota(jnp.int32, (lanes, width), 1)
         for sector in range(SECTORS_HERE):
-            for part in range(X_PART):
-                low = part * rows + first_row[piece]
-                start = (sector * X_PART + part) * count
-                out[sector, low : low + count, chunk * lanes : (chunk + 1) * lanes] = value[
-                    start : start + count
-                ]
+            keep = (row < widths[0, sector]) & (column < widths[1, sector])
+            block = value[:, sector * LANES : sector * LANES + width]
+            out[sector, chunk * lanes : (chunk + 1) * lanes, :] = jnp.where(keep, block, 0.0)
 
     first_parts()
     for part in range(2):
@@ -435,34 +456,34 @@
     spread(2)
     chain(0, 0)
     spread(3)
+    make_spots()
     chain(0, 1)
     chain(0, 2)
     gather(1)
     chain(0, 3)
     forward(2)
     chain(1, 0)
+    forward(3)
     finish(0)
     chain(1, 1)
-    forward(3)
-    put(0)
     chain(1, 2)
     gather(2)
+    chain(2, 0)
     chain(1, 3)
-    chain(2, 0)
+    put(0)
     gather(3)
+    chain(2, 1)
+    chain(3, 0)
+    chain(2, 2)
+    chain(3, 1)
     finish(1)
-    chain(3, 0)
-    chain(2, 1)
-    chain(3, 1)
-    put(1)
-    chain(2, 2)
     chain(3, 2)
     chain(2, 3)
     chain(3, 3)
+    put(1)
     finish(2)
     finish(3)
     put(2)
-    put(3)
 
     for dy in range(1, NY):
         order_copy(dy).wait_send()
@@ -487,7 +508,6 @@
     size = psi.shape[1]
     targets = pair_src.shape[1]
     rows, lanes = size // SLOTS, size // CHUNKS
-    term = lax.axis_index("term")
     bf, count = jnp.bfloat16, len(PIECES)
     tile = (TILE, lanes)
     scratch = [
@@ -514,6 +534,7 @@
             ring, ring, ring, ring,
             pltpu.VMEM((X_PART, here // 2) + tile, bf),
             pltpu.VMEM((X_PART, here // 2) + tile, bf),
+            pltpu.VMEM((X_PART * here * SECTORS_HERE, SECTORS_HERE * LANES), bf),
         ]
     dma = pltpu.SemaphoreType.DMA
     scratch += [
@@ -522,9 +543,9 @@
         dma((count, STEPS)), dma((count, STEPS)), dma((count, STEPS)), dma((count, STEPS)),
         dma((count, X_PART)), dma((count,)),
     ]
-    summed = pl.pallas_call(
+    return pl.pallas_call(
         kernel,
-        out_shape=jax.ShapeDtypeStruct((SECTORS_HERE, X_PART * rows, size), jnp.float32),
+        out_shape=jax.ShapeDtypeStruct((SECTORS_HERE, size, X_PART * rows), jnp.float32),
         in_specs=[
             pl.BlockSpec(memory_space=pltpu.VMEM),
             pl.BlockSpec(memory_space=pltpu.SMEM),
@@ -542,14 +563,6 @@
         ),
     )(pair_src, widths, psi, left_ops, right_ops)
 
-    summed = jnp.swapaxes(summed, 1, 2)
-    line = jnp.arange(size, dtype=jnp.int32)
-    columns = term * (X_PART * rows) + jnp.arange(X_PART * rows, dtype=jnp.int32)
-    keep = (line[None, :, None] < widths[0][:, None, None]) & (
-        columns[None, None, :] < widths[1][:, None, None]
-    )
-    return jnp.where(keep, summed, jnp.zeros_like(summed))
-
 
 def solution(mesh):
     return jax.shard_map(

time: 96 us -> 96.2 us (level)
  other arithmetic: 2.16 us -> 0 us
  local copies, waits for them, and re-layouts: 0.76 us -> 2.67 us
    pallas_call x0 -> x1, local copies, waits for them, and re-layouts: none -> 2.67 us  [shards(): pl.pallas_call(kernel, out_shape=jax.ShapeDtypeStruct((SECTORS_HERE, size...]
    select_n x1 -> x0, other arithmetic: 2.01 us -> none  [shards(): return jnp.where(keep, summed, jnp.zeros_like(summed))]
where the time goes in v5:
time: 96.2 us; the launch traced here: 96 us
  Pallas kernels  93.3 us (97%)
  local copies, waits for them, and re-layouts  2.67 us (3%)
    pallas_call x1, Pallas kernels, shards(): pl.pallas_call(kernel, out_shape=jax.ShapeDtypeStruct((SECTORS_HERE, size...  93.3 us
    pallas_call x1, local copies, waits for them, and re-layouts, shards(): pl.pallas_call(kernel, out_shape=jax.ShapeDtypeStruct((SECTORS_HERE, size...  2.67 us

profile of v5, /device:TPU:1, one launch (start us, length us, event | category | flops | bytes accessed | tf_op | source)
XLA Modules:
  0.0 96.0 jit_solution(16019931836924954064)
XLA Ops:
  0.0 93.3 %shard_map.55 = f32[8,384,48]{2,1,0:T(8,128)} custom-call(s32[2,256]{1,0:T(2,128)} %pair_src.1, s32[2,8]{1,0:T(2,128)} %widths.1, bf16[8,384,384]{2,1,0:T(8,128)(2,1)} %psi.1, bf16[2,8,384,384]{3,2,1,0:T(8,128)(2,1)} %left.1, bf16[2,8,384,384]{3,2,1,0:T(8,128)(2,1)} %right.1), custom_call_target="tpu_custom_call" | custom-call | flops 3623878656 | bytes 11796480 | tf_op jit(solution)/shard_map/pallas_call | solution.py:546
  93.4 2.7 %copy.6 = f32[8,384,48]{1,2,0:T(8,128)} copy(f32[8,384,48]{2,1,0:T(8,128)} %shard_map.55) | data formatting | bytes 1179648 | tf_op jit(solution)/shard_map/pallas_call | solution.py:546

commit v6 on v4

--- a/solution.py
+++ b/solution.py
@@ -16,23 +16,12 @@
 X_PART = NX // NC
 STEPS = NZ // 2
 MESH = pl.DeviceIdType.MESH
-BUFFERS = 11
-
-
-def routes(sign):
-    direct, relayed = [], []
-    for dx in range(NX):
-        for dy in range(NY):
-            far_x, far_y = NX > 2 and dx == NX // 2, NY > 2 and dy == NY // 2
-            if far_x or far_y:
-                via = (sign if far_x else 0, sign if far_y else 0)
-                relayed.append(((dx, dy), via, (dx - via[0], dy - via[1])))
-            elif (dx, dy) != (0, 0):
-                direct.append((dx, dy))
-    return direct, relayed
-
-
-RELAYS = len(routes(1)[1])
+BUFFERS = 10
+
+
+def moves():
+    every = [(dx, dy) for dx in range(NX) for dy in range(NY) if (dx, dy) != (0, 0)]
+    return sorted(every, key=lambda move: -min(move[0], NX - move[0]) - min(move[1], NY - move[1]))
 
 
 def device(x, y, z, c):
@@ -52,10 +41,10 @@
     sends, rest = rest[:CHUNKS], rest[CHUNKS:]
     buffers = [rest[i * BUFFERS : (i + 1) * BUFFERS] for i in range(len(PIECES))]
     (
-        load_sem, order_sem, order_send, spread_send, spread_recv, relay_recv, relay_send, core_send, core_recv,
+        load_sem, order_sem, order_send, spread_send, spread_recv, core_send, core_recv,
         up_send, up_recv, down_send, down_recv, final_send, final_recv,
     ) = rest[len(PIECES) * BUFFERS :]
-    got, relay, give, take, own, up_out, up_in, down_out, down_in, done, final = zip(*buffers)
+    got, give, take, own, up_out, up_in, down_out, down_in, done, final = zip(*buffers)
     sec, term = lax.axis_index("sec"), lax.axis_index("term")
     x, z = lax.div(sec, NZ), lax.rem(sec, NZ)
     y, c = lax.div(term, NC), lax.rem(term, NC)
@@ -72,12 +61,7 @@
         return lax.rem(value + (by % count), count)
 
     barrier = pltpu.get_barrier_semaphore()
-    others = [
-        device(shifted(x, dx, NX), shifted(y, dy, NY), z, c)
-        for dx in range(NX)
-        for dy in range(NY)
-        if (dx, dy) != (0, 0)
-    ]
+    others = [device(shifted(x, dx, NX), shifted(y, dy, NY), z, c) for dx, dy in moves()]
     others += [device(shifted(x, dx, NX), y, z, 1 - c) for dx in range(NX)]
     others += [device(x, y, shifted(z, 1, NZ), c), device(x, y, shifted(z, -1, NZ), c)]
     for other in others:
@@ -194,7 +178,7 @@
 
     def halves(piece):
         count = piece_rows[piece] // 2
-        return ((0, 1, 0, count), (1, -1, count, count))
+        return ((1, 0, count), (-1, count, count))
 
     def block_for(piece, x_to, y_to, low, count):
         start = (y_to * NX + x_to) * rows + first_row[piece] + low
@@ -204,19 +188,8 @@
         return got[piece].at[low : low + count, tile_at(y_from * NX + x_from)]
 
     def spread(piece, rings=range(NY)):
-        for half, sign, low, count in halves(piece):
-            for j, ((dx, dy), (vx, vy), _) in enumerate(routes(sign)[1]):
-                if dy in rings:
-                    pltpu.make_async_remote_copy(
-                        src_ref=block_for(piece, shifted(x, dx, NX), shifted(y, dy, NY), low, count),
-                        dst_ref=relay[piece].at[half, j],
-                        send_sem=spread_send.at[piece],
-                        recv_sem=relay_recv.at[piece, half],
-                        device_id=device(shifted(x, vx, NX), shifted(y, vy, NY), z, c),
-                        device_id_type=MESH,
-                    ).start()
         count = piece_rows[piece]
-        for dx, dy in routes(1)[0]:
+        for dx, dy in moves():
             if dy in rings:
                 xd, yd = shifted(x, dx, NX), shifted(y, dy, NY)
                 pltpu.make_async_remote_copy(
@@ -231,22 +204,6 @@
             pltpu.make_async_copy(
                 block_for(piece, x, y, 0, count), place(piece, x, y, 0, count), spread_recv.at[piece]
             ).start()
-
-    def forward(piece):
-        if RELAYS == 0:
-            return
-        for half, sign, low, count in halves(piece):
-            arrived = relay[piece].at[half]
-            pltpu.make_async_copy(arrived, arrived, relay_recv.at[piece, half]).wait()
-            for j, (_, (vx, vy), (fx, fy)) in enumerate(routes(sign)[1]):
-                pltpu.make_async_remote_copy(
-                    src_ref=relay[piece].at[half, j],
-                    dst_ref=place(piece, shifted(x, -vx, NX), shifted(y, -vy, NY), low, count),
-                    send_sem=relay_send.at[piece],
-                    recv_sem=spread_recv.at[piece],
-                    device_id=device(shifted(x, fx, NX), shifted(y, fy, NY), z, c),
-                    device_id_type=MESH,
-                ).start()
 
     def order_copy(dy):
         return pltpu.make_async_remote_copy(
@@ -322,7 +279,7 @@
         out_sem, in_sem = (up_send, up_recv) if way > 0 else (down_send, down_recv)
         at = (step,)
         if step == 0:
-            _, _, low, count = halves(piece)[0 if way > 0 else 1]
+            _, low, count = halves(piece)[0 if way > 0 else 1]
             at = (step, slice(low, low + count))
         return pltpu.make_async_remote_copy(
             src_ref=source.at[at],
@@ -346,7 +303,7 @@
             if step > 0:
                 z_copy(piece, step - 1, way).wait_recv()
             zd = shifted(z, way * (STEPS - step), NZ)
-            for _, sign, low, count in halves(piece):
+            for sign, low, count in halves(piece):
                 if carried(step, way, sign):
                     at = slice(low, low + count)
                     value = held(piece, zd, low, count)
@@ -373,7 +330,7 @@
         last = STEPS - 1
         for way in (1, -1):
             z_copy(piece, last, way).wait_recv()
-        for _, sign, low, count in halves(piece):
+        for sign, low, count in halves(piece):
             value = held(piece, z, low, count)
             for way in (1, -1):
                 if carried(last, way, sign):
@@ -426,39 +383,35 @@
         order_copy(dy).start()
     pltpu.make_async_copy(orders_own, orders.at[y], order_sem.at[0]).start()
     later_parts()
-    forward(0)
     later_images()
     spread(1)
+    spread(2)
+    spread(3)
     make_pick()
     gather(0)
-    forward(1)
-    spread(2)
     chain(0, 0)
-    spread(3)
     chain(0, 1)
     chain(0, 2)
+    chain(0, 3)
+    finish(0)
     gather(1)
-    chain(0, 3)
-    forward(2)
     chain(1, 0)
-    finish(0)
     chain(1, 1)
-    forward(3)
     put(0)
     chain(1, 2)
     gather(2)
+    chain(2, 0)
     chain(1, 3)
-    chain(2, 0)
     gather(3)
+    chain(2, 1)
+    chain(3, 0)
+    chain(2, 2)
+    chain(3, 1)
     finish(1)
-    chain(3, 0)
-    chain(2, 1)
-    chain(3, 1)
-    put(1)
-    chain(2, 2)
     chain(3, 2)
     chain(2, 3)
     chain(3, 3)
+    put(1)
     finish(2)
     finish(3)
     put(2)
@@ -469,8 +422,6 @@
     for piece in pieces:
         sent = sends[PIECES[piece][0]].at[0 : (SLOTS - 1) * piece_rows[piece]]
         pltpu.make_async_copy(sent, sent, spread_send.at[piece]).wait()
-        if RELAYS:
-            pltpu.make_async_copy(relay[piece], relay[piece], relay_send.at[piece]).wait()
         core_copy(piece).wait_send()
         for step in range(STEPS):
             for way in (1, -1):
@@ -507,7 +458,6 @@
         ring = pltpu.VMEM((STEPS, here) + tile, bf)
         scratch += [
             pltpu.VMEM((here, SOURCES, lanes), bf),
-            pltpu.VMEM((2, max(RELAYS, 1), here // 2) + tile, bf),
             pltpu.VMEM((NZ, here) + tile, bf),
             pltpu.VMEM((NZ, here) + tile, bf),
             pltpu.VMEM((NZ, here) + tile, jnp.float32),
@@ -518,7 +468,7 @@
     dma = pltpu.SemaphoreType.DMA
     scratch += [
         dma((3, SECTORS_HERE)), dma((1,)), dma((NY,)), dma((count,)), dma((count,)),
-        dma((count, 2)), dma((count,)), dma((count,)), dma((count,)),
+        dma((count,)), dma((count,)),
         dma((count, STEPS)), dma((count, STEPS)), dma((count, STEPS)), dma((count, STEPS)),
         dma((count, X_PART)), dma((count,)),
     ]

time: 96 us -> 104 us (1.083)
  Pallas kernels: 92.9 us -> 101 us
    pallas_call x1, Pallas kernels: 92.9 us -> 101 us  [shards(): pl.pallas_call(kernel, out_shape=jax.ShapeDtypeStruct((SECTORS_HERE, X_PA...]
where the time goes in v6:
time: 104 us
  Pallas kernels  101 us (97%)
  other arithmetic  2.16 us (2%)
    pallas_call x1, Pallas kernels, shards(): pl.pallas_call(kernel, out_shape=jax.ShapeDtypeStruct((SECTORS_HERE, X_PA...  101 us

profile of v6, /device:TPU:1, one launch (start us, length us, event | category | flops | bytes accessed | tf_op | source)
XLA Modules:
  0.0 104.2 jit_solution(10712734626550450677)
XLA Ops:
  0.0 0.8 slice_bitcast_fusion.1
  0.8 0.1 broadcast_compare_fusion
  0.8 0.1 iota_compare_fusion
  0.9 101.3 %shard_map.55 = f32[8,48,384]{2,1,0:T(8,128)} custom-call(s32[2,256]{1,0:T(2,128)} %pair_src.1, s32[2,8]{1,0:T(2,128)} %widths.1, bf16[8,384,384]{2,1,0:T(8,128)(2,1)} %psi.1, bf16[2,8,384,384]{3,2,1,0:T(8,128)(2,1)} %left.1, bf16[2,8,384,384]{3,2,1,0:T(8,128)(2,1)} %right.1), custom_call_target="tpu_custom_call" | custom-call | flops 3623878656 | bytes 11796480 | tf_op jit(solution)/shard_map/pallas_call | solution.py:475
  102.2 2.0 %bitcast_select_fusion = f32[8,384,48]{1,2,0:T(8,128)} fusion(f32[8,48,384]{2,1,0:T(8,128)} %shard_map.55, pred[8,48]{1,0:T(8,128)(4,1)S(1)} %broadcast_compare_fusion, pred[8,384]{1,0:T(8,128)(4,1)S(1)} %iota_compare_fusion), kind=kLoop, calls=%fused_computation | loop fusion | flops 294912 | bytes 1183104 | tf_op jit(solution)/shard_map/jit(_where)/select_n | solution.py:501
  (1 shorter events, 0.0 us)

commit v7 on v6

--- a/solution.py
+++ b/solution.py
@@ -16,12 +16,28 @@
 X_PART = NX // NC
 STEPS = NZ // 2
 MESH = pl.DeviceIdType.MESH
-BUFFERS = 10
-
-
-def moves():
-    every = [(dx, dy) for dx in range(NX) for dy in range(NY) if (dx, dy) != (0, 0)]
-    return sorted(every, key=lambda move: -min(move[0], NX - move[0]) - min(move[1], NY - move[1]))
+BUFFERS = 11
+
+
+def places():
+    found = []
+    for dx in range(NX):
+        for dy in range(NY):
+            if (dx, dy) != (0, 0):
+                found.append((dx, dy, NX > 2 and dx == NX // 2, NY > 2 and dy == NY // 2))
+    return sorted(found, key=lambda at: -min(at[0], NX - at[0]) - min(at[1], NY - at[1]))
+
+
+def relayed():
+    found = []
+    for dx, dy, far_x, far_y in places():
+        if far_x or far_y:
+            via = (1 if far_x else 0, 1 if far_y else 0)
+            found.append(((dx, dy), via, (dx - via[0], dy - via[1])))
+    return found
+
+
+RELAYS = len(relayed())
 
 
 def device(x, y, z, c):
@@ -41,10 +57,10 @@
     sends, rest = rest[:CHUNKS], rest[CHUNKS:]
     buffers = [rest[i * BUFFERS : (i + 1) * BUFFERS] for i in range(len(PIECES))]
     (
-        load_sem, order_sem, order_send, spread_send, spread_recv, core_send, core_recv,
+        load_sem, order_sem, order_send, spread_send, spread_recv, relay_recv, relay_send, core_send, core_recv,
         up_send, up_recv, down_send, down_recv, final_send, final_recv,
     ) = rest[len(PIECES) * BUFFERS :]
-    got, give, take, own, up_out, up_in, down_out, down_in, done, final = zip(*buffers)
+    got, relay, give, take, own, up_out, up_in, down_out, down_in, done, final = zip(*buffers)
     sec, term = lax.axis_index("sec"), lax.axis_index("term")
     x, z = lax.div(sec, NZ), lax.rem(sec, NZ)
     y, c = lax.div(term, NC), lax.rem(term, NC)
@@ -61,7 +77,7 @@
         return lax.rem(value + (by % count), count)
 
     barrier = pltpu.get_barrier_semaphore()
-    others = [device(shifted(x, dx, NX), shifted(y, dy, NY), z, c) for dx, dy in moves()]
+    others = [device(shifted(x, dx, NX), shifted(y, dy, NY), z, c) for dx, dy, _, _ in places()]
     others += [device(shifted(x, dx, NX), y, z, 1 - c) for dx in range(NX)]
     others += [device(x, y, shifted(z, 1, NZ), c), device(x, y, shifted(z, -1, NZ), c)]
     for other in others:
@@ -116,36 +132,6 @@
 
         each_sector(one)
 
-    def first_images(rings, first):
-        count = size // NY
-        starts = [pl.multiple_of(shifted(y, dy, NY) * count, 2 * TILE) for dy in rings]
-
-        def one(k):
-            if first:
-                loads(k)[2].wait()
-            for group in range(GROUPS_HERE):
-                chosen = jnp.concatenate([right_v[group, k, pl.ds(start, count), :] for start in starts], 0)
-                image[group * SECTORS_HERE + k, 0 : count * len(starts), 0:lanes] = image_of(
-                    chosen, parts[k, group * lanes : (group + 1) * lanes, :]
-                )
-
-        each_sector(one)
-        for low in range(0, count * len(starts), 2 * TILE):
-            both = turned(
-                jnp.concatenate(
-                    [
-                        image[:, at : at + TILE, 0:lanes].reshape(TILE * TILE, lanes)
-                        for at in (low, low + TILE)
-                    ],
-                    1,
-                )
-            )
-            for part in range(2):
-                at = starts[low // count] + low % count + part * TILE
-                sends[0][pl.ds(at, TILE)] = both[:, part * lanes : (part + 1) * lanes].reshape(
-                    TILE, TILE, lanes
-                )
-
     later = size - lanes
 
     def later_parts():
@@ -155,26 +141,33 @@
 
         each_sector(one)
 
-    def later_images():
+    def images(rings, chunks, wait):
+        count = size // NY
+        width = lanes * len(chunks)
+        starts = [pl.multiple_of(shifted(y, dy, NY) * count, 2 * TILE) for dy in rings]
+
         def one(k):
+            if wait:
+                loads(k)[2].wait()
             for group in range(GROUPS_HERE):
-                image[group * SECTORS_HERE + k] = image_of(
-                    right_v[group, k], parts[k, group * later : (group + 1) * later, :]
+                chosen = jnp.concatenate([right_v[group, k, pl.ds(start, count), :] for start in starts], 0)
+                image[group * SECTORS_HERE + k, 0 : count * len(starts), 0:width] = image_of(
+                    chosen, parts[k, group * width : (group + 1) * width, :]
                 )
 
         each_sector(one)
-
-        def some(step, _):
-            for inner in range(4):
-                at = pl.multiple_of((step * 4 + inner) * TILE, TILE)
-                value = turned(image[:, pl.ds(at, TILE), :].reshape(TILE * TILE, later))
-                for chunk in range(1, CHUNKS):
-                    sends[chunk][pl.ds(at, TILE)] = value[
-                        :, (chunk - 1) * lanes : chunk * lanes
-                    ].reshape(TILE, TILE, lanes)
-            return 0
-
-        lax.fori_loop(0, size // (4 * TILE), some, 0)
+        step = 2 // len(chunks)
+        for low in range(0, count * len(starts), step * TILE):
+            blocks = [
+                image[:, low + part * TILE : low + (part + 1) * TILE, 0:width].reshape(TILE * TILE, width)
+                for part in range(step)
+            ]
+            value = turned(blocks[0] if step == 1 else jnp.concatenate(blocks, 1))
+            for part in range(2):
+                at = starts[low // count] + low % count + (part * TILE if step == 2 else 0)
+                sends[chunks[0 if step == 2 else part]][pl.ds(at, TILE)] = value[
+                    :, part * lanes : (part + 1) * lanes
+                ].reshape(TILE, TILE, lanes)
 
     def halves(piece):
         count = piece_rows[piece] // 2
@@ -189,12 +182,25 @@
 
     def spread(piece, rings=range(NY)):
         count = piece_rows[piece]
-        for dx, dy in moves():
+        for j, ((dx, dy), (vx, vy), _) in enumerate(relayed()):
+            if dy in rings:
+                pltpu.make_async_remote_copy(
+                    src_ref=block_for(
+                        piece, shifted(x, dx, NX), shifted(y, dy, NY), count // 2, count // 2
+                    ),
+                    dst_ref=relay[piece].at[j],
+                    send_sem=spread_send.at[piece],
+                    recv_sem=relay_recv.at[piece],
+                    device_id=device(shifted(x, vx, NX), shifted(y, vy, NY), z, c),
+                    device_id_type=MESH,
+                ).start()
+        for dx, dy, far_x, far_y in places():
             if dy in rings:
                 xd, yd = shifted(x, dx, NX), shifted(y, dy, NY)
+                straight = count // 2 if far_x or far_y else count
                 pltpu.make_async_remote_copy(
-                    src_ref=block_for(piece, xd, yd, 0, count),
-                    dst_ref=place(piece, x, y, 0, count),
+                    src_ref=block_for(piece, xd, yd, 0, straight),
+                    dst_ref=place(piece, x, y, 0, straight),
                     send_sem=spread_send.at[piece],
                     recv_sem=spread_recv.at[piece],
                     device_id=device(xd, yd, z, c),
@@ -203,6 +209,21 @@
         if 0 in rings:
             pltpu.make_async_copy(
                 block_for(piece, x, y, 0, count), place(piece, x, y, 0, count), spread_recv.at[piece]
+            ).start()
+
+    def forward(piece):
+        if RELAYS == 0:
+            return
+        count = piece_rows[piece] // 2
+        pltpu.make_async_copy(relay[piece], relay[piece], relay_recv.at[piece]).wait()
+        for j, (_, (vx, vy), (fx, fy)) in enumerate(relayed()):
+            pltpu.make_async_remote_copy(
+                src_ref=relay[piece].at[j],
+                dst_ref=place(piece, shifted(x, -vx, NX), shifted(y, -vy, NY), count, count),
+                send_sem=relay_send.at[piece],
+                recv_sem=spread_recv.at[piece],
+                device_id=device(shifted(x, fx, NX), shifted(y, fy, NY), z, c),
+                device_id_type=MESH,
             ).start()
 
     def order_copy(dy):
@@ -373,29 +394,34 @@
                 ]
 
     first_parts()
-    for part in range(2):
-        rings = y_order[part * NY // 2 : (part + 1) * NY // 2]
-        first_images(rings, part == 0)
-        if part == 0:
+    ring_halves = (y_order[: NY // 2], y_order[NY // 2 :])
+    for rings in ring_halves:
+        images(rings, (0,), rings is ring_halves[0])
+        if rings is ring_halves[0]:
             pl.semaphore_wait(barrier, len(others))
         spread(0, rings)
     for dy in range(1, NY):
         order_copy(dy).start()
     pltpu.make_async_copy(orders_own, orders.at[y], order_sem.at[0]).start()
     later_parts()
-    later_images()
-    spread(1)
-    spread(2)
-    spread(3)
+    forward(0)
+    for rings in ring_halves:
+        images(rings, (1, 2), False)
+        spread(1, rings)
     make_pick()
     gather(0)
+    forward(1)
+    spread(2)
     chain(0, 0)
     chain(0, 1)
+    spread(3)
     chain(0, 2)
+    gather(1)
     chain(0, 3)
+    forward(2)
+    chain(1, 0)
+    forward(3)
     finish(0)
-    gather(1)
-    chain(1, 0)
     chain(1, 1)
     put(0)
     chain(1, 2)
@@ -422,6 +448,8 @@
     for piece in pieces:
         sent = sends[PIECES[piece][0]].at[0 : (SLOTS - 1) * piece_rows[piece]]
         pltpu.make_async_copy(sent, sent, spread_send.at[piece]).wait()
+        if RELAYS:
+            pltpu.make_async_copy(relay[piece], relay[piece], relay_send.at[piece]).wait()
         core_copy(piece).wait_send()
         for step in range(STEPS):
             for way in (1, -1):
@@ -458,6 +486,7 @@
         ring = pltpu.VMEM((STEPS, here) + tile, bf)
         scratch += [
             pltpu.VMEM((here, SOURCES, lanes), bf),
+            pltpu.VMEM((max(RELAYS, 1), here // 2) + tile, bf),
             pltpu.VMEM((NZ, here) + tile, bf),
             pltpu.VMEM((NZ, here) + tile, bf),
             pltpu.VMEM((NZ, here) + tile, jnp.float32),
@@ -468,7 +497,7 @@
     dma = pltpu.SemaphoreType.DMA
     scratch += [
         dma((3, SECTORS_HERE)), dma((1,)), dma((NY,)), dma((count,)), dma((count,)),
-        dma((count,)), dma((count,)),
+        dma((count,)), dma((count,)), dma((count,)), dma((count,)),
         dma((count, STEPS)), dma((count, STEPS)), dma((count, STEPS)), dma((count, STEPS)),
         dma((count, X_PART)), dma((count,)),
     ]

time: 104 us -> 111 us (1.067)
  Pallas kernels: 101 us -> 107 us
    pallas_call x1, Pallas kernels: 101 us -> 107 us  [shards(): pl.pallas_call(kernel, out_shape=jax.ShapeDtypeStruct((SECTORS_HERE, X_PA...]
where the time goes in v7:
time: 111 us; the launch traced here: 110 us
  Pallas kernels  107 us (96%)
  other arithmetic  2.16 us (2%)
    pallas_call x1, Pallas kernels, shards(): pl.pallas_call(kernel, out_shape=jax.ShapeDtypeStruct((SECTORS_HERE, X_PA...  107 us

profile of v7, /device:TPU:1, one launch (start us, length us, event | category | flops | bytes accessed | tf_op | source)
XLA Modules:
  0.0 110.2 jit_solution(13563284242833528472)
XLA Ops:
  0.0 0.8 slice_bitcast_fusion.1
  0.8 0.1 broadcast_compare_fusion
  0.8 0.1 iota_compare_fusion
  0.9 107.3 %shard_map.55 = f32[8,48,384]{2,1,0:T(8,128)} custom-call(s32[2,256]{1,0:T(2,128)} %pair_src.1, s32[2,8]{1,0:T(2,128)} %widths.1, bf16[8,384,384]{2,1,0:T(8,128)(2,1)} %psi.1, bf16[2,8,384,384]{3,2,1,0:T(8,128)(2,1)} %left.1, bf16[2,8,384,384]{3,2,1,0:T(8,128)(2,1)} %right.1), custom_call_target="tpu_custom_call" | custom-call | flops 3623878656 | bytes 11796480 | tf_op jit(solution)/shard_map/pallas_call | solution.py:504
  108.2 2.0 %bitcast_select_fusion = f32[8,384,48]{1,2,0:T(8,128)} fusion(f32[8,48,384]{2,1,0:T(8,128)} %shard_map.55, pred[8,48]{1,0:T(8,128)(4,1)S(1)} %broadcast_compare_fusion, pred[8,384]{1,0:T(8,128)(4,1)S(1)} %iota_compare_fusion), kind=kLoop, calls=%fused_computation | loop fusion | flops 294912 | bytes 1183104 | tf_op jit(solution)/shard_map/jit(_where)/select_n | solution.py:530
  (1 shorter events, 0.0 us)

commit v8 on v4

--- a/solution.py
+++ b/solution.py
@@ -132,36 +132,6 @@
 
         each_sector(one)
 
-    def first_images(rings, first):
-        count = size // NY
-        starts = [pl.multiple_of(shifted(y, dy, NY) * count, 2 * TILE) for dy in rings]
-
-        def one(k):
-            if first:
-                loads(k)[2].wait()
-            for group in range(GROUPS_HERE):
-                chosen = jnp.concatenate([right_v[group, k, pl.ds(start, count), :] for start in starts], 0)
-                image[group * SECTORS_HERE + k, 0 : count * len(starts), 0:lanes] = image_of(
-                    chosen, parts[k, group * lanes : (group + 1) * lanes, :]
-                )
-
-        each_sector(one)
-        for low in range(0, count * len(starts), 2 * TILE):
-            both = turned(
-                jnp.concatenate(
-                    [
-                        image[:, at : at + TILE, 0:lanes].reshape(TILE * TILE, lanes)
-                        for at in (low, low + TILE)
-                    ],
-                    1,
-                )
-            )
-            for part in range(2):
-                at = starts[low // count] + low % count + part * TILE
-                sends[0][pl.ds(at, TILE)] = both[:, part * lanes : (part + 1) * lanes].reshape(
-                    TILE, TILE, lanes
-                )
-
     later = size - lanes
 
     def later_parts():
@@ -171,26 +141,30 @@
 
         each_sector(one)
 
-    def later_images():
+    def images(chunk):
         def one(k):
+            if chunk == 0:
+                loads(k)[2].wait()
             for group in range(GROUPS_HERE):
+                low = group * lanes if chunk == 0 else group * later + (chunk - 1) * lanes
                 image[group * SECTORS_HERE + k] = image_of(
-                    right_v[group, k], parts[k, group * later : (group + 1) * later, :]
+                    right_v[group, k], parts[k, low : low + lanes, :]
                 )
 
         each_sector(one)
 
-        def some(step, _):
-            for inner in range(4):
-                at = pl.multiple_of((step * 4 + inner) * TILE, TILE)
-                value = turned(image[:, pl.ds(at, TILE), :].reshape(TILE * TILE, later))
-                for chunk in range(1, CHUNKS):
-                    sends[chunk][pl.ds(at, TILE)] = value[
-                        :, (chunk - 1) * lanes : chunk * lanes
+    def turn(chunk, rings):
+        count = size // NY
+        for dy in rings:
+            start = shifted(y, dy, NY) * count
+            for low in range(0, count, 2 * TILE):
+                at = [pl.multiple_of(start + low + part * TILE, TILE) for part in range(2)]
+                blocks = [image[:, pl.ds(here, TILE), :].reshape(TILE * TILE, lanes) for here in at]
+                value = turned(jnp.concatenate(blocks, 1))
+                for part in range(2):
+                    sends[chunk][pl.ds(at[part], TILE)] = value[
+                        :, part * lanes : (part + 1) * lanes
                     ].reshape(TILE, TILE, lanes)
-            return 0
-
-        lax.fori_loop(0, size // (4 * TILE), some, 0)
 
     def halves(piece):
         count = piece_rows[piece] // 2
@@ -415,22 +389,27 @@
                     start : start + count
                 ]
 
+    ring_halves = (y_order[: NY // 2], y_order[NY // 2 :])
     first_parts()
-    for part in range(2):
-        rings = y_order[part * NY // 2 : (part + 1) * NY // 2]
-        first_images(rings, part == 0)
-        if part == 0:
-            pl.semaphore_wait(barrier, len(others))
-        spread(0, rings)
+    images(0)
+    turn(0, ring_halves[0])
+    pl.semaphore_wait(barrier, len(others))
+    spread(0, ring_halves[0])
+    turn(0, ring_halves[1])
+    spread(0, ring_halves[1])
     for dy in range(1, NY):
         order_copy(dy).start()
     pltpu.make_async_copy(orders_own, orders.at[y], order_sem.at[0]).start()
     later_parts()
     forward(0)
-    later_images()
-    spread(1)
+    images(1)
+    for rings in ring_halves:
+        turn(1, rings)
+        spread(1, rings)
+    images(2)
     make_pick()
     gather(0)
+    turn(2, range(NY))
     forward(1)
     spread(2)
     chain(0, 0)
@@ -441,24 +420,24 @@
     chain(0, 3)
     forward(2)
     chain(1, 0)
+    forward(3)
     finish(0)
     chain(1, 1)
-    forward(3)
     put(0)
     chain(1, 2)
     gather(2)
+    chain(2, 0)
     chain(1, 3)
-    chain(2, 0)
     gather(3)
+    chain(2, 1)
+    chain(3, 0)
+    chain(2, 2)
+    chain(3, 1)
     finish(1)
-    chain(3, 0)
-    chain(2, 1)
-    chain(3, 1)
-    put(1)
-    chain(2, 2)
     chain(3, 2)
     chain(2, 3)
     chain(3, 3)
+    put(1)
     finish(2)
     finish(3)
     put(2)
@@ -497,7 +476,7 @@
         pltpu.VMEM((8, targets), jnp.int32),
         pltpu.VMEM((NY, 8, targets), jnp.int32),
         pltpu.VMEM((SECTORS_HERE, GROUPS_HERE * (size - lanes), size), bf),
-        pltpu.VMEM((TILE, size, size - lanes), bf),
+        pltpu.VMEM((TILE, size, lanes), bf),
         pltpu.VMEM((TILE * TILE, TILE * TILE), bf),
         pltpu.VMEM((targets, SOURCES), bf),
         *[pltpu.VMEM((size,) + tile, bf) for _ in range(CHUNKS)],

time: 96 us -> 98.6 us (1.027)
  Pallas kernels: 92.9 us -> 95.5 us
    pallas_call x1, Pallas kernels: 92.9 us -> 95.5 us  [shards(): pl.pallas_call(kernel, out_shape=jax.ShapeDtypeStruct((SECTORS_HERE, X_PA...]
where the time goes in v8:
time: 98.6 us; the launch traced here: 98.4 us
  Pallas kernels  95.5 us (97%)
  other arithmetic  2.16 us (2%)
    pallas_call x1, Pallas kernels, shards(): pl.pallas_call(kernel, out_shape=jax.ShapeDtypeStruct((SECTORS_HERE, X_PA...  95.5 us
    select_n x1, other arithmetic, shards(): return jnp.where(keep, summed, jnp.zeros_like(summed))  2.01 us

profile of v8, /device:TPU:1, one launch (start us, length us, event | category | flops | bytes accessed | tf_op | source)
XLA Modules:
  0.0 98.4 jit_solution(10848424918206286705)
XLA Ops:
  0.0 0.8 slice_bitcast_fusion.1
  0.8 0.1 broadcast_compare_fusion
  0.8 0.1 iota_compare_fusion
  0.9 95.5 %shard_map.55 = f32[8,48,384]{2,1,0:T(8,128)} custom-call(s32[2,256]{1,0:T(2,128)} %pair_src.1, s32[2,8]{1,0:T(2,128)} %widths.1, bf16[8,384,384]{2,1,0:T(8,128)(2,1)} %psi.1, bf16[2,8,384,384]{3,2,1,0:T(8,128)(2,1)} %left.1, bf16[2,8,384,384]{3,2,1,0:T(8,128)(2,1)} %right.1), custom_call_target="tpu_custom_call" | custom-call | flops 3623878656 | bytes 11796480 | tf_op jit(solution)/shard_map/pallas_call | solution.py:504
  96.4 2.0 %bitcast_select_fusion = f32[8,384,48]{1,2,0:T(8,128)} fusion(f32[8,48,384]{2,1,0:T(8,128)} %shard_map.55, pred[8,48]{1,0:T(8,128)(4,1)S(1)} %broadcast_compare_fusion, pred[8,384]{1,0:T(8,128)(4,1)S(1)} %iota_compare_fusion), kind=kLoop, calls=%fused_computation | loop fusion | flops 294912 | bytes 1183104 | tf_op jit(solution)/shard_map/jit(_where)/select_n | solution.py:530
  (1 shorter events, 0.0 us)

commit v9 on v4

--- a/solution.py
+++ b/solution.py
@@ -16,6 +16,7 @@
 X_PART = NX // NC
 STEPS = NZ // 2
 MESH = pl.DeviceIdType.MESH
+LAST = len(PIECES) - 1
 BUFFERS = 11
 
 
@@ -53,7 +54,8 @@
     buffers = [rest[i * BUFFERS : (i + 1) * BUFFERS] for i in range(len(PIECES))]
     (
         load_sem, order_sem, order_send, spread_send, spread_recv, relay_recv, relay_send, core_send, core_recv,
-        up_send, up_recv, down_send, down_recv, final_send, final_recv,
+        up_send, up_recv, down_send, down_recv, final_send, final_recv, straight_send, straight_recv,
+        straight_out, straight_in,
     ) = rest[len(PIECES) * BUFFERS :]
     got, relay, give, take, own, up_out, up_in, down_out, down_in, done, final = zip(*buffers)
     sec, term = lax.axis_index("sec"), lax.axis_index("term")
@@ -79,18 +81,23 @@
         if (dx, dy) != (0, 0)
     ]
     others += [device(shifted(x, dx, NX), y, z, 1 - c) for dx in range(NX)]
-    others += [device(x, y, shifted(z, 1, NZ), c), device(x, y, shifted(z, -1, NZ), c)]
+    others += [device(x, y, shifted(z, dz, NZ), c) for dz in range(1, NZ)]
     for other in others:
         pl.semaphore_signal(barrier, inc=1, device_id=other, device_id_type=MESH)
 
     def loads(k):
         return (
             pltpu.make_async_copy(psi.at[k], psi_v.at[k], load_sem.at[0, k]),
-            pltpu.make_async_copy(left.at[:, k], left_v.at[:, k], load_sem.at[1, k]),
+            pltpu.make_async_copy(
+                left.at[:, k, 0:lanes], left_v.at[:, k, 0:lanes], load_sem.at[1, k]
+            ),
             pltpu.make_async_copy(right.at[:, k], right_v.at[:, k], load_sem.at[2, k]),
-        )
-
-    for which in ((0, 1), (2,)):
+            pltpu.make_async_copy(
+                left.at[:, k, lanes:size], left_v.at[:, k, lanes:size], load_sem.at[3, k]
+            ),
+        )
+
+    for which in ((0, 1), (2,), (3,)):
         for k in range(SECTORS_HERE):
             for copy in which:
                 loads(k)[copy].start()
@@ -166,6 +173,7 @@
 
     def later_parts():
         def one(k):
+            loads(k)[3].wait()
             here = left_v[:, k, lanes:, :].reshape(GROUPS_HERE * later, size)
             parts[k] = jnp.dot(here, psi_v[k], preferred_element_type=jnp.float32).astype(jnp.bfloat16)
 
@@ -204,7 +212,7 @@
         return got[piece].at[low : low + count, tile_at(y_from * NX + x_from)]
 
     def spread(piece, rings=range(NY)):
-        for half, sign, low, count in halves(piece):
+        for half, sign, low, count in halves(piece) if piece != LAST else ():
             for j, ((dx, dy), (vx, vy), _) in enumerate(routes(sign)[1]):
                 if dy in rings:
                     pltpu.make_async_remote_copy(
@@ -216,7 +224,7 @@
                         device_id_type=MESH,
                     ).start()
         count = piece_rows[piece]
-        for dx, dy in routes(1)[0]:
+        for dx, dy in routes(1)[0] + ([route[0] for route in routes(1)[1]] if piece == LAST else []):
             if dy in rings:
                 xd, yd = shifted(x, dx, NX), shifted(y, dy, NY)
                 pltpu.make_async_remote_copy(
@@ -333,6 +341,23 @@
             device_id_type=MESH,
         )
 
+    def straight_copy(dz):
+        return pltpu.make_async_remote_copy(
+            src_ref=straight_out.at[dz - 1],
+            dst_ref=straight_in.at[dz - 1],
+            send_sem=straight_send.at[dz - 1],
+            recv_sem=straight_recv.at[0],
+            device_id=device(x, y, shifted(z, dz, NZ), c),
+            device_id_type=MESH,
+        )
+
+    def straight():
+        core_copy(LAST).wait_recv()
+        for dz in sorted(range(1, NZ), key=lambda dz: -min(dz, NZ - dz)):
+            value = held(LAST, shifted(z, dz, NZ), 0, piece_rows[LAST])
+            straight_out[dz - 1] = value.astype(jnp.bfloat16)
+            straight_copy(dz).start()
+
     def carried(step, way, sign):
         return step > 0 or way == sign
 
@@ -371,11 +396,17 @@
 
     def finish(piece):
         last = STEPS - 1
-        for way in (1, -1):
-            z_copy(piece, last, way).wait_recv()
+        if piece == LAST:
+            pltpu.make_async_copy(straight_in, straight_in, straight_recv.at[0]).wait()
+        else:
+            for way in (1, -1):
+                z_copy(piece, last, way).wait_recv()
         for _, sign, low, count in halves(piece):
             value = held(piece, z, low, count)
-            for way in (1, -1):
+            if piece == LAST:
+                for dz in range(1, NZ):
+                    value = value + straight_in[dz - 1, low : low + count].astype(jnp.float32)
+            for way in (1, -1) if piece != LAST else ():
                 if carried(last, way, sign):
                     value = value + z_buffers(piece, way)[1][last, low : low + count].astype(jnp.float32)
             for part in range(X_PART):
@@ -411,9 +442,12 @@
             for part in range(X_PART):
                 low = part * rows + first_row[piece]
                 start = (sector * X_PART + part) * count
-                out[sector, low : low + count, chunk * lanes : (chunk + 1) * lanes] = value[
-                    start : start + count
-                ]
+                m = term * (X_PART * rows) + low + lax.broadcasted_iota(jnp.int32, (count, lanes), 0)
+                i = chunk * lanes + lax.broadcasted_iota(jnp.int32, (count, lanes), 1)
+                keep = (i < widths[0, sector]) & (m < widths[1, sector])
+                out[sector, low : low + count, chunk * lanes : (chunk + 1) * lanes] = jnp.where(
+                    keep, value[start : start + count], 0.0
+                )
 
     first_parts()
     for part in range(2):
@@ -443,36 +477,34 @@
     chain(1, 0)
     finish(0)
     chain(1, 1)
-    forward(3)
     put(0)
     chain(1, 2)
     gather(2)
+    chain(2, 0)
     chain(1, 3)
-    chain(2, 0)
     gather(3)
+    chain(2, 1)
+    straight()
     finish(1)
-    chain(3, 0)
-    chain(2, 1)
-    chain(3, 1)
+    chain(2, 2)
+    chain(2, 3)
     put(1)
-    chain(2, 2)
-    chain(3, 2)
-    chain(2, 3)
-    chain(3, 3)
+    finish(3)
     finish(2)
-    finish(3)
+    put(3)
     put(2)
-    put(3)
 
     for dy in range(1, NY):
         order_copy(dy).wait_send()
+    for dz in range(1, NZ):
+        straight_copy(dz).wait_send()
     for piece in pieces:
         sent = sends[PIECES[piece][0]].at[0 : (SLOTS - 1) * piece_rows[piece]]
         pltpu.make_async_copy(sent, sent, spread_send.at[piece]).wait()
-        if RELAYS:
+        if RELAYS and piece != LAST:
             pltpu.make_async_copy(relay[piece], relay[piece], relay_send.at[piece]).wait()
         core_copy(piece).wait_send()
-        for step in range(STEPS):
+        for step in range(STEPS) if piece != LAST else ():
             for way in (1, -1):
                 z_copy(piece, step, way).wait_send()
         for part in range(X_PART):
@@ -487,7 +519,6 @@
     size = psi.shape[1]
     targets = pair_src.shape[1]
     rows, lanes = size // SLOTS, size // CHUNKS
-    term = lax.axis_index("term")
     bf, count = jnp.bfloat16, len(PIECES)
     tile = (TILE, lanes)
     scratch = [
@@ -517,10 +548,11 @@
         ]
     dma = pltpu.SemaphoreType.DMA
     scratch += [
-        dma((3, SECTORS_HERE)), dma((1,)), dma((NY,)), dma((count,)), dma((count,)),
+        dma((4, SECTORS_HERE)), dma((1,)), dma((NY,)), dma((count,)), dma((count,)),
         dma((count, 2)), dma((count,)), dma((count,)), dma((count,)),
         dma((count, STEPS)), dma((count, STEPS)), dma((count, STEPS)), dma((count, STEPS)),
-        dma((count, X_PART)), dma((count,)),
+        dma((count, X_PART)), dma((count,)), dma((NZ - 1,)), dma((1,)),
+        *[pltpu.VMEM((NZ - 1, rows * PIECES[LAST][2] // 3) + tile, bf) for _ in range(2)],
     ]
     summed = pl.pallas_call(
         kernel,
@@ -542,13 +574,7 @@
         ),
     )(pair_src, widths, psi, left_ops, right_ops)
 
-    summed = jnp.swapaxes(summed, 1, 2)
-    line = jnp.arange(size, dtype=jnp.int32)
-    columns = term * (X_PART * rows) + jnp.arange(X_PART * rows, dtype=jnp.int32)
-    keep = (line[None, :, None] < widths[0][:, None, None]) & (
-        columns[None, None, :] < widths[1][:, None, None]
-    )
-    return jnp.where(keep, summed, jnp.zeros_like(summed))
+    return jnp.swapaxes(summed, 1, 2)
 
 
 def solution(mesh):

time: 96 us -> 96.1 us (level)
  other arithmetic: 2.16 us -> 0 us
  local copies, waits for them, and re-layouts: 0.76 us -> 1.92 us
  Pallas kernels: 92.9 us -> 94 us
    select_n x1 -> x0, other arithmetic: 2.01 us -> none  [shards(): return jnp.where(keep, summed, jnp.zeros_like(summed))]
    unnamed x0 -> x1, local copies, waits for them, and re-layouts: none -> 1.92 us
    pallas_call x1, Pallas kernels: 92.9 us -> 94 us  [shards(): pl.pallas_call(kernel, out_shape=jax.ShapeDtypeStruct((SECTORS_HERE, X_PA...]
where the time goes in v9:
time: 96.1 us; the launch traced here: 95.9 us
  Pallas kernels  94 us (98%)
  local copies, waits for them, and re-layouts  1.92 us (2%)
    pallas_call x1, Pallas kernels, shards(): pl.pallas_call(kernel, out_shape=jax.ShapeDtypeStruct((SECTORS_HERE, X_PA...  94 us

profile of v9, /device:TPU:1, one launch (start us, length us, event | category | flops | bytes accessed | tf_op | source)
XLA Modules:
  0.0 95.9 jit_solution(6368377525842413720)
XLA Ops:
  0.0 94.0 %shard_map.55 = f32[8,48,384]{2,1,0:T(8,128)} custom-call(s32[2,256]{1,0:T(2,128)} %pair_src.1, s32[2,8]{1,0:T(2,128)} %widths.1, bf16[8,384,384]{2,1,0:T(8,128)(2,1)} %psi.1, bf16[2,8,384,384]{3,2,1,0:T(8,128)(2,1)} %left.1, bf16[2,8,384,384]{3,2,1,0:T(8,128)(2,1)} %right.1), custom_call_target="tpu_custom_call" | custom-call | flops 3623878656 | bytes 11796480 | tf_op jit(solution)/shard_map/pallas_call | solution.py:557
  94.0 1.9 %copy.7 = f32[8,384,48]{1,2,0:T(8,128)} copy(f32[8,384,48]{1,2,0:T(8,128)} %bitcast.1) | data formatting | bytes 1179648

commit v10 on v4

--- a/solution.py
+++ b/solution.py
@@ -16,6 +16,7 @@
 X_PART = NX // NC
 STEPS = NZ // 2
 MESH = pl.DeviceIdType.MESH
+LAST = len(PIECES) - 1
 BUFFERS = 11
 
 
@@ -86,11 +87,16 @@
     def loads(k):
         return (
             pltpu.make_async_copy(psi.at[k], psi_v.at[k], load_sem.at[0, k]),
-            pltpu.make_async_copy(left.at[:, k], left_v.at[:, k], load_sem.at[1, k]),
+            pltpu.make_async_copy(
+                left.at[:, k, 0:lanes], left_v.at[:, k, 0:lanes], load_sem.at[1, k]
+            ),
             pltpu.make_async_copy(right.at[:, k], right_v.at[:, k], load_sem.at[2, k]),
+            pltpu.make_async_copy(
+                left.at[:, k, lanes:size], left_v.at[:, k, lanes:size], load_sem.at[3, k]
+            ),
         )
 
-    for which in ((0, 1), (2,)):
+    for which in ((0, 1), (2,), (3,)):
         for k in range(SECTORS_HERE):
             for copy in which:
                 loads(k)[copy].start()
@@ -166,6 +172,7 @@
 
     def later_parts():
         def one(k):
+            loads(k)[3].wait()
             here = left_v[:, k, lanes:, :].reshape(GROUPS_HERE * later, size)
             parts[k] = jnp.dot(here, psi_v[k], preferred_element_type=jnp.float32).astype(jnp.bfloat16)
 
@@ -204,7 +211,7 @@
         return got[piece].at[low : low + count, tile_at(y_from * NX + x_from)]
 
     def spread(piece, rings=range(NY)):
-        for half, sign, low, count in halves(piece):
+        for half, sign, low, count in halves(piece) if piece != LAST else ():
             for j, ((dx, dy), (vx, vy), _) in enumerate(routes(sign)[1]):
                 if dy in rings:
                     pltpu.make_async_remote_copy(
@@ -216,7 +223,7 @@
                         device_id_type=MESH,
                     ).start()
         count = piece_rows[piece]
-        for dx, dy in routes(1)[0]:
+        for dx, dy in ([route[0] for route in routes(1)[1]] if piece == LAST else []) + routes(1)[0]:
             if dy in rings:
                 xd, yd = shifted(x, dx, NX), shifted(y, dy, NY)
                 pltpu.make_async_remote_copy(
@@ -411,9 +418,12 @@
             for part in range(X_PART):
                 low = part * rows + first_row[piece]
                 start = (sector * X_PART + part) * count
-                out[sector, low : low + count, chunk * lanes : (chunk + 1) * lanes] = value[
-                    start : start + count
-                ]
+                m = term * (X_PART * rows) + low + lax.broadcasted_iota(jnp.int32, (count, lanes), 0)
+                i = chunk * lanes + lax.broadcasted_iota(jnp.int32, (count, lanes), 1)
+                keep = (i < widths[0, sector]) & (m < widths[1, sector])
+                out[sector, low : low + count, chunk * lanes : (chunk + 1) * lanes] = jnp.where(
+                    keep, value[start : start + count], 0.0
+                )
 
     first_parts()
     for part in range(2):
@@ -443,7 +453,6 @@
     chain(1, 0)
     finish(0)
     chain(1, 1)
-    forward(3)
     put(0)
     chain(1, 2)
     gather(2)
@@ -469,7 +478,7 @@
     for piece in pieces:
         sent = sends[PIECES[piece][0]].at[0 : (SLOTS - 1) * piece_rows[piece]]
         pltpu.make_async_copy(sent, sent, spread_send.at[piece]).wait()
-        if RELAYS:
+        if RELAYS and piece != LAST:
             pltpu.make_async_copy(relay[piece], relay[piece], relay_send.at[piece]).wait()
         core_copy(piece).wait_send()
         for step in range(STEPS):
@@ -487,7 +496,6 @@
     size = psi.shape[1]
     targets = pair_src.shape[1]
     rows, lanes = size // SLOTS, size // CHUNKS
-    term = lax.axis_index("term")
     bf, count = jnp.bfloat16, len(PIECES)
     tile = (TILE, lanes)
     scratch = [
@@ -517,7 +525,7 @@
         ]
     dma = pltpu.SemaphoreType.DMA
     scratch += [
-        dma((3, SECTORS_HERE)), dma((1,)), dma((NY,)), dma((count,)), dma((count,)),
+        dma((4, SECTORS_HERE)), dma((1,)), dma((NY,)), dma((count,)), dma((count,)),
         dma((count, 2)), dma((count,)), dma((count,)), dma((count,)),
         dma((count, STEPS)), dma((count, STEPS)), dma((count, STEPS)), dma((count, STEPS)),
         dma((count, X_PART)), dma((count,)),
@@ -542,13 +550,7 @@
         ),
     )(pair_src, widths, psi, left_ops, right_ops)
 
-    summed = jnp.swapaxes(summed, 1, 2)
-    line = jnp.arange(size, dtype=jnp.int32)
-    columns = term * (X_PART * rows) + jnp.arange(X_PART * rows, dtype=jnp.int32)
-    keep = (line[None, :, None] < widths[0][:, None, None]) & (
-        columns[None, None, :] < widths[1][:, None, None]
-    )
-    return jnp.where(keep, summed, jnp.zeros_like(summed))
+    return jnp.swapaxes(summed, 1, 2)
 
 
 def solution(mesh):

time: 96 us -> 96.4 us (level)
  other arithmetic: 2.16 us -> 0 us
  Pallas kernels: 92.9 us -> 94.3 us
  local copies, waits for them, and re-layouts: 0.76 us -> 1.92 us
    select_n x1 -> x0, other arithmetic: 2.01 us -> none  [shards(): return jnp.where(keep, summed, jnp.zeros_like(summed))]
    unnamed x0 -> x1, local copies, waits for them, and re-layouts: none -> 1.92 us
    pallas_call x1, Pallas kernels: 92.9 us -> 94.3 us  [shards(): pl.pallas_call(kernel, out_shape=jax.ShapeDtypeStruct((SECTORS_HERE, X_PA...]
where the time goes in v10:
time: 96.4 us; the launch traced here: 96.3 us
  Pallas kernels  94.3 us (98%)
  local copies, waits for them, and re-layouts  1.92 us (2%)
    pallas_call x1, Pallas kernels, shards(): pl.pallas_call(kernel, out_shape=jax.ShapeDtypeStruct((SECTORS_HERE, X_PA...  94.3 us

profile of v10, /device:TPU:1, one launch (start us, length us, event | category | flops | bytes accessed | tf_op | source)
XLA Modules:
  0.0 96.3 jit_solution(15849403973509785769)
XLA Ops:
  0.0 94.3 %shard_map.55 = f32[8,48,384]{2,1,0:T(8,128)} custom-call(s32[2,256]{1,0:T(2,128)} %pair_src.1, s32[2,8]{1,0:T(2,128)} %widths.1, bf16[8,384,384]{2,1,0:T(8,128)(2,1)} %psi.1, bf16[2,8,384,384]{3,2,1,0:T(8,128)(2,1)} %left.1, bf16[2,8,384,384]{3,2,1,0:T(8,128)(2,1)} %right.1), custom_call_target="tpu_custom_call" | custom-call | flops 3623878656 | bytes 11796480 | tf_op jit(solution)/shard_map/pallas_call | solution.py:533
  94.3 1.9 %copy.7 = f32[8,384,48]{1,2,0:T(8,128)} copy(f32[8,384,48]{1,2,0:T(8,128)} %bitcast.1) | data formatting | bytes 1179648

commit v11 on v10

--- a/solution.py
+++ b/solution.py
@@ -16,7 +16,6 @@
 X_PART = NX // NC
 STEPS = NZ // 2
 MESH = pl.DeviceIdType.MESH
-LAST = len(PIECES) - 1
 BUFFERS = 11
 
 
@@ -211,7 +210,7 @@
         return got[piece].at[low : low + count, tile_at(y_from * NX + x_from)]
 
     def spread(piece, rings=range(NY)):
-        for half, sign, low, count in halves(piece) if piece != LAST else ():
+        for half, sign, low, count in halves(piece):
             for j, ((dx, dy), (vx, vy), _) in enumerate(routes(sign)[1]):
                 if dy in rings:
                     pltpu.make_async_remote_copy(
@@ -223,7 +222,7 @@
                         device_id_type=MESH,
                     ).start()
         count = piece_rows[piece]
-        for dx, dy in ([route[0] for route in routes(1)[1]] if piece == LAST else []) + routes(1)[0]:
+        for dx, dy in routes(1)[0]:
             if dy in rings:
                 xd, yd = shifted(x, dx, NX), shifted(y, dy, NY)
                 pltpu.make_async_remote_copy(
@@ -426,12 +425,11 @@
                 )
 
     first_parts()
-    for part in range(2):
-        rings = y_order[part * NY // 2 : (part + 1) * NY // 2]
-        first_images(rings, part == 0)
-        if part == 0:
-            pl.semaphore_wait(barrier, len(others))
-        spread(0, rings)
+    first_images(y_order[:1], True)
+    pl.semaphore_wait(barrier, len(others))
+    spread(0, y_order[:1])
+    first_images(y_order[1:], False)
+    spread(0, y_order[1:])
     for dy in range(1, NY):
         order_copy(dy).start()
     pltpu.make_async_copy(orders_own, orders.at[y], order_sem.at[0]).start()
@@ -453,6 +451,7 @@
     chain(1, 0)
     finish(0)
     chain(1, 1)
+    forward(3)
     put(0)
     chain(1, 2)
     gather(2)
@@ -478,7 +477,7 @@
     for piece in pieces:
         sent = sends[PIECES[piece][0]].at[0 : (SLOTS - 1) * piece_rows[piece]]
         pltpu.make_async_copy(sent, sent, spread_send.at[piece]).wait()
-        if RELAYS and piece != LAST:
+        if RELAYS:
             pltpu.make_async_copy(relay[piece], relay[piece], relay_send.at[piece]).wait()
         core_copy(piece).wait_send()
         for step in range(STEPS):

time: 96.4 us -> 94.8 us (0.983)
  Pallas kernels: 94.3 us -> 92.7 us
    pallas_call x1, Pallas kernels: 94.3 us -> 92.7 us  [shards(): pl.pallas_call(kernel, out_shape=jax.ShapeDtypeStruct((SECTORS_HERE, X_PA...]
where the time goes in v11:
time: 94.8 us; the launch traced here: 94.6 us
  Pallas kernels  92.7 us (98%)
  local copies, waits for them, and re-layouts  1.92 us (2%)
    pallas_call x1, Pallas kernels, shards(): pl.pallas_call(kernel, out_shape=jax.ShapeDtypeStruct((SECTORS_HERE, X_PA...  92.7 us
    unnamed x1, local copies, waits for them, and re-layouts  1.92 us

profile of v11, /device:TPU:1, one launch (start us, length us, event | category | flops | bytes accessed | tf_op | source)
XLA Modules:
  0.0 94.6 jit_solution(7788626143272462686)
XLA Ops:
  0.0 92.7 %shard_map.55 = f32[8,48,384]{2,1,0:T(8,128)} custom-call(s32[2,256]{1,0:T(2,128)} %pair_src.1, s32[2,8]{1,0:T(2,128)} %widths.1, bf16[8,384,384]{2,1,0:T(8,128)(2,1)} %psi.1, bf16[2,8,384,384]{3,2,1,0:T(8,128)(2,1)} %left.1, bf16[2,8,384,384]{3,2,1,0:T(8,128)(2,1)} %right.1), custom_call_target="tpu_custom_call" | custom-call | flops 3623878656 | bytes 11796480 | tf_op jit(solution)/shard_map/pallas_call | solution.py:532
  92.7 1.9 %copy.7 = f32[8,384,48]{1,2,0:T(8,128)} copy(f32[8,384,48]{1,2,0:T(8,128)} %bitcast.1) | data formatting | bytes 1179648

commit v12 on v11

--- a/solution.py
+++ b/solution.py
@@ -186,9 +186,13 @@
 
         each_sector(one)
 
+    def later_turn(dy):
+        count = size // NY
+        start = shifted(y, dy, NY) * count
+
         def some(step, _):
-            for inner in range(4):
-                at = pl.multiple_of((step * 4 + inner) * TILE, TILE)
+            for inner in range(3):
+                at = pl.multiple_of(start + (step * 3 + inner) * TILE, TILE)
                 value = turned(image[:, pl.ds(at, TILE), :].reshape(TILE * TILE, later))
                 for chunk in range(1, CHUNKS):
                     sends[chunk][pl.ds(at, TILE)] = value[
@@ -196,7 +200,7 @@
                     ].reshape(TILE, TILE, lanes)
             return 0
 
-        lax.fori_loop(0, size // (4 * TILE), some, 0)
+        lax.fori_loop(0, count // (3 * TILE), some, 0)
 
     def halves(piece):
         count = piece_rows[piece] // 2
@@ -436,7 +440,11 @@
     later_parts()
     forward(0)
     later_images()
-    spread(1)
+    for part in range(2):
+        rings = y_order[part * NY // 2 : (part + 1) * NY // 2]
+        for dy in rings:
+            later_turn(dy)
+        spread(1, rings)
     make_pick()
     gather(0)
     forward(1)

time: 94.8 us -> 95.7 us (level)
  Pallas kernels: 92.7 us -> 93.7 us
    pallas_call x1, Pallas kernels: 92.7 us -> 93.7 us  [shards(): pl.pallas_call(kernel, out_shape=jax.ShapeDtypeStruct((SECTORS_HERE, X_PA...]
where the time goes in v12:
time: 95.7 us; the launch traced here: 95.6 us
  Pallas kernels  93.7 us (98%)
  local copies, waits for them, and re-layouts  1.92 us (2%)
    pallas_call x1, Pallas kernels, shards(): pl.pallas_call(kernel, out_shape=jax.ShapeDtypeStruct((SECTORS_HERE, X_PA...  93.7 us
    unnamed x1, local copies, waits for them, and re-layouts  1.92 us

profile of v12, /device:TPU:1, one launch (start us, length us, event | category | flops | bytes accessed | tf_op | source)
XLA Modules:
  0.0 95.6 jit_solution(5325485679136970937)
XLA Ops:
  0.0 93.7 %shard_map.55 = f32[8,48,384]{2,1,0:T(8,128)} custom-call(s32[2,256]{1,0:T(2,128)} %pair_src.1, s32[2,8]{1,0:T(2,128)} %widths.1, bf16[8,384,384]{2,1,0:T(8,128)(2,1)} %psi.1, bf16[2,8,384,384]{3,2,1,0:T(8,128)(2,1)} %left.1, bf16[2,8,384,384]{3,2,1,0:T(8,128)(2,1)} %right.1), custom_call_target="tpu_custom_call" | custom-call | flops 3623878656 | bytes 11796480 | tf_op jit(solution)/shard_map/pallas_call | solution.py:540
  93.7 1.9 %copy.7 = f32[8,384,48]{1,2,0:T(8,128)} copy(f32[8,384,48]{1,2,0:T(8,128)} %bitcast.1) | data formatting | bytes 1179648

commit v13 on v11

--- a/solution.py
+++ b/solution.py
@@ -210,8 +210,9 @@
         return got[piece].at[low : low + count, tile_at(y_from * NX + x_from)]
 
     def spread(piece, rings=range(NY)):
-        for half, sign, low, count in halves(piece):
-            for j, ((dx, dy), (vx, vy), _) in enumerate(routes(sign)[1]):
+        for j in range(RELAYS):
+            for half, sign, low, count in halves(piece):
+                (dx, dy), (vx, vy), _ = routes(sign)[1][j]
                 if dy in rings:
                     pltpu.make_async_remote_copy(
                         src_ref=block_for(piece, shifted(x, dx, NX), shifted(y, dy, NY), low, count),
@@ -241,10 +242,12 @@
     def forward(piece):
         if RELAYS == 0:
             return
-        for half, sign, low, count in halves(piece):
+        for half in range(2):
             arrived = relay[piece].at[half]
             pltpu.make_async_copy(arrived, arrived, relay_recv.at[piece, half]).wait()
-            for j, (_, (vx, vy), (fx, fy)) in enumerate(routes(sign)[1]):
+        for j in range(RELAYS):
+            for half, sign, low, count in halves(piece):
+                _, (vx, vy), (fx, fy) = routes(sign)[1][j]
                 pltpu.make_async_remote_copy(
                     src_ref=relay[piece].at[half, j],
                     dst_ref=place(piece, shifted(x, -vx, NX), shifted(y, -vy, NY), low, count),

time: 94.8 us -> 94.8 us (level)
  no operation moved by 1% of the time
where the time goes in v13:
time: 94.8 us; the launch traced here: 94.6 us
  Pallas kernels  92.7 us (98%)
  local copies, waits for them, and re-layouts  1.92 us (2%)
    pallas_call x1, Pallas kernels, shards(): pl.pallas_call(kernel, out_shape=jax.ShapeDtypeStruct((SECTORS_HERE, X_PA...  92.7 us
    unnamed x1, local copies, waits for them, and re-layouts  1.92 us

profile of v13, /device:TPU:1, one launch (start us, length us, event | category | flops | bytes accessed | tf_op | source)
XLA Modules:
  0.0 94.6 jit_solution(18119726755304315039)
XLA Ops:
  0.0 92.7 %shard_map.55 = f32[8,48,384]{2,1,0:T(8,128)} custom-call(s32[2,256]{1,0:T(2,128)} %pair_src.1, s32[2,8]{1,0:T(2,128)} %widths.1, bf16[8,384,384]{2,1,0:T(8,128)(2,1)} %psi.1, bf16[2,8,384,384]{3,2,1,0:T(8,128)(2,1)} %left.1, bf16[2,8,384,384]{3,2,1,0:T(8,128)(2,1)} %right.1), custom_call_target="tpu_custom_call" | custom-call | flops 3623878656 | bytes 11796480 | tf_op jit(solution)/shard_map/pallas_call | solution.py:535
  92.7 1.9 %copy.7 = f32[8,384,48]{1,2,0:T(8,128)} copy(f32[8,384,48]{1,2,0:T(8,128)} %bitcast.1) | data formatting | bytes 1179648
